TPU v7x, 32 devices: a whole 2x2x4 slice. The times are simulated.
32 devices in a mesh: fsdp: 4 (over z), ctx: 2 (over x), tp: 4 (over y, core).
Axes of the slice: x: 2, y: 2, z: 4, core: 2. Of those that a mesh axis runs over, the one named last changes fastest.
Arguments:
- tokens: bfloat16 [4, 1024, 1024], P('fsdp', 'ctx'), may hold values from -16 to 16
- segments: int32 [4, 1024], P('fsdp'), may hold values from 0 to 1023, as said below
- w_qkv: bfloat16 [1024, 3, 1024], P(('fsdp', 'ctx'), None, 'tp'), may hold values from -0.1875 to 0.1875
- b_qv: bfloat16 [2, 16, 64], P(None, 'tp', ('fsdp', 'ctx')), may hold values from -0.59765625 to 0.59765625
- w_out: bfloat16 [1024, 1024], P('tp', ('fsdp', 'ctx')), may hold values from -0.75 to 0.75
- b_out: bfloat16 [1024], P(('fsdp', 'ctx')), may hold values from -3 to 3
- w_up: bfloat16 [1024, 4096], P(('fsdp', 'ctx'), 'tp'), may hold values from -0.1875 to 0.1875
- b_up: bfloat16 [64, 64], P('tp', ('fsdp', 'ctx')), may hold values from -3 to 3
- w_down: bfloat16 [4096, 1024], P('tp', ('fsdp', 'ctx')), may hold values from -0.09375 to 0.09375
- b_down: bfloat16 [1024], P(('fsdp', 'ctx')), may hold values from -3 to 3
- attngain: bfloat16 [1024], P(('fsdp', 'ctx')), may hold values from 0.5 to 1.5
- attnshift: bfloat16 [1024], P(('fsdp', 'ctx')), may hold values from -3 to 3
- mlpgain: bfloat16 [1024], P(('fsdp', 'ctx')), may hold values from 0.5 to 1.5
- mlpshift: bfloat16 [1024], P(('fsdp', 'ctx')), may hold values from -3 to 3
- cotangent: bfloat16 [4, 1024, 1024], P('fsdp', 'ctx'), may hold values from -6 to 6
Outputs:
- block_out: bfloat16 [4, 1024, 1024], P('fsdp', 'ctx')
- grad_tokens: float32 [4, 1024, 1024], P('fsdp', 'ctx')
- grad_wqkv: float32 [1024, 3, 1024], P(('fsdp', 'ctx'), None, 'tp')
- grad_bqv: float32 [2, 16, 64], P(None, 'tp', ('fsdp', 'ctx'))
- grad_wout: float32 [1024, 1024], P('tp', ('fsdp', 'ctx'))
- grad_bout: float32 [1024], P(('fsdp', 'ctx'))
- grad_wup: float32 [1024, 4096], P(('fsdp', 'ctx'), 'tp')
- grad_bup: float32 [64, 64], P('tp', ('fsdp', 'ctx'))
- grad_wdown: float32 [4096, 1024], P('tp', ('fsdp', 'ctx'))
- grad_bdown: float32 [1024], P(('fsdp', 'ctx'))
- grad_attngain: float32 [1024], P(('fsdp', 'ctx'))
- grad_attnshift: float32 [1024], P(('fsdp', 'ctx'))
- grad_mlpgain: float32 [1024], P(('fsdp', 'ctx'))
- grad_mlpshift: float32 [1024], P(('fsdp', 'ctx'))
Inputs may be any that keep to these rules, and one draw needn't show every extreme that they name: `segments`: in each sequence the numbers start at 0 and never fall along it; equal numbers mark one document; the last document of every sequence has the number 1024 - 1.
All inputs are finite; a program needn't handle non-finite values.
Results may differ from a plain program's by a relative error of at most 0.018.
Values may be sent and summed in bfloat16 or wider, within the bound.
No kernel may reach another device: no remote copies, remote signals or barrier semaphores. Data moves between devices by JAX's collectives and lax.ppermute only.
A program may use at most 128 MiB of HBM per device.

v0:
```python
import functools

import jax
import jax.numpy as jnp
from jax import lax
from jax.experimental import pallas as pl
from jax.experimental.layout import Layout, with_layout_constraint
from jax.experimental.pallas import tpu as pltpu
from jax.sharding import PartitionSpec as P

HD = 64
LANES = 128
CORE = 1
CHIP = 2
VMEM_LIMIT = 16 * 1024 * 1024

epsilon = 1e-05
negative = -1e30


def swap(array, axis, mask=1):
    devices = lax.axis_size(axis)
    return lax.ppermute(array, axis, [(i, i ^ mask) for i in range(devices)])


def ordered(place, own, other):
    return jnp.where(place == 0, own, other), jnp.where(place == 0, other, own)


def gather_fsdp(block):
    devices = lax.axis_size("fsdp")
    return lax.all_to_all(
        jnp.broadcast_to(block[None], (devices,) + block.shape), "fsdp", 0, 0, tiled=True
    )


def gather_rows(block):
    return lax.all_gather(block, "fsdp", axis=0, tiled=True)


def row_major(array):
    return with_layout_constraint(array, Layout(tuple(range(array.ndim))))


def sum_tp(part_of, rows, core_place, work=None, gated=()):
    half = rows // 2
    sent = swap(part_of((1 - core_place) * half, half).astype(jnp.bfloat16), "tp", CORE)
    kept = part_of(core_place * half, half)
    chip_sum = (kept + sent.astype(jnp.float32)).astype(jnp.bfloat16)
    chip_sum, gated = lax.optimization_barrier((chip_sum, gated))
    across = swap(chip_sum, "tp", CHIP)
    done, free = work(gated, chip_sum) if work else ((), ())
    across, done = lax.optimization_barrier((across, done))
    total = (chip_sum.astype(jnp.float32) + across.astype(jnp.float32)).astype(jnp.bfloat16)
    summed = jnp.concatenate(ordered(core_place, total, swap(total, "tp", CORE)), axis=0)
    return summed, done, free


def other_tokens(rows, core_place):
    half = rows.shape[0] // 2
    got = swap(lax.dynamic_slice_in_dim(rows, core_place * half, half, 0), "ctx")
    return got, swap(got, "tp", CORE)


def chip_sum_rows(sent, kept, right):
    sent = swap(dot(sent, right, 1, 1).astype(jnp.bfloat16), "tp", CORE)
    return (dot(kept, right, 1, 1) + sent.astype(jnp.float32)).astype(jnp.bfloat16)


def chip_parts(own, other, right, core_place):
    half = own.shape[0] // 2
    return (
        chip_sum_rows(
            lax.dynamic_slice_in_dim(own, (1 - core_place) * half, half, 0),
            lax.dynamic_slice_in_dim(own, core_place * half, half, 0),
            right,
        ),
        chip_sum_rows(other[half:], other[:half], right),
    )


def weight_product(wide, narrow, ctx_place):
    devices = lax.axis_size("fsdp")
    rows = wide.shape[1] // (devices * 2)
    product = dot(wide, narrow, 0, 0).astype(jnp.bfloat16).reshape(devices, 2, rows, -1)
    return tuple(
        part.reshape(devices * rows, -1)
        for part in ordered(ctx_place, product[:, 0], product[:, 1])
    )


def pair_sum(kept, sent):
    return (kept.astype(jnp.float32) + sent.astype(jnp.float32)).astype(jnp.bfloat16)


def scatter_rows(array):
    return lax.psum_scatter(array, "fsdp", scatter_dimension=0, tiled=True)


def normalize(matrix, factor, offset):
    average = jnp.mean(matrix, axis=-1, keepdims=True)
    centered = matrix - average
    spread = jnp.mean(centered * centered, axis=-1, keepdims=True)
    return centered * lax.rsqrt(spread + epsilon) * factor + offset


def normalize_back(matrix, factor, grad):
    average = jnp.mean(matrix, axis=-1, keepdims=True)
    centered = matrix - average
    spread = jnp.mean(centered * centered, axis=-1, keepdims=True)
    inverse = lax.rsqrt(spread + epsilon)
    xhat = centered * inverse
    scaled = grad * factor
    mean_scaled = jnp.mean(scaled, axis=-1, keepdims=True)
    mean_product = jnp.mean(scaled * xhat, axis=-1, keepdims=True)
    grad_in = inverse * (scaled - mean_scaled - xhat * mean_product)
    return grad_in, jnp.sum(grad * xhat, axis=0), jnp.sum(grad, axis=0)


def gelu_tanh(inputs):
    cubed_vals = inputs * inputs * inputs
    return 0.5 * inputs * (1.0 + jnp.tanh(0.7978845608028654 * (inputs + 0.044715 * cubed_vals)))


def dot(left, right, left_dim, right_dim):
    return lax.dot_general(
        left, right, (((left_dim,), (right_dim,)), ((), ())), preferred_element_type=jnp.float32
    )


def head_masks(shape):
    lane = lax.broadcasted_iota(jnp.int32, shape, 1)
    return [(lane // HD) == head for head in range(shape[1] // HD)]


def attend_kernel(
    rows, drow, scale,
    tokens_ref, packs_ref, vectors_ref, bias_ref, seg_row_ref, seg_col_ref,
    normed_ref, qkv_ref, attended_ref, weight_ref, out_ref,
):
    length = tokens_ref.shape[0]
    part = attended_ref.shape[1]
    for owner in range(packs_ref.shape[0]):
        for kind in range(3):
            weight_ref[owner * drow : (owner + 1) * drow, kind * part : (kind + 1) * part] = (
                packs_ref[owner, kind * drow : (kind + 1) * drow, :]
            )
        for side in range(2):
            first = packs_ref.shape[1] - (2 - side) * drow
            out_ref[owner * drow : (owner + 1) * drow, side * part : (side + 1) * part] = (
                packs_ref[owner, first : first + drow, :]
            )
    masks = head_masks((rows, part))
    for block in range(length // rows):
        here = slice(block * rows, (block + 1) * rows)
        seen = (block + 1) * rows
        inputs = tokens_ref[here, :].astype(jnp.float32)
        centered = inputs - jnp.mean(inputs, axis=-1, keepdims=True)
        spread = jnp.mean(centered * centered, axis=-1, keepdims=True)
        normed = (
            centered * lax.rsqrt(spread + epsilon) * vectors_ref[0:1, :] + vectors_ref[1:2, :]
        ).astype(jnp.bfloat16)
        normed_ref[here, :] = normed
        projected = dot(normed, weight_ref[...], 1, 0) + bias_ref[...]
        qkv_ref[here, :] = projected.astype(jnp.bfloat16)
        queries = qkv_ref[here, :part]
        key_rows = qkv_ref[:seen, part : 2 * part]
        value_rows = qkv_ref[:seen, 2 * part :]
        query_index = block * rows + lax.broadcasted_iota(jnp.int32, (rows, seen), 0)
        key_index = lax.broadcasted_iota(jnp.int32, (rows, seen), 1)
        allowed = (seg_col_ref[here, :] == seg_row_ref[:, :seen]) & (key_index <= query_index)
        result = jnp.zeros((rows, part), jnp.float32)
        for mask in masks:
            scores = dot(jnp.where(mask, queries, 0), key_rows, 1, 1) * scale
            scores = jnp.where(allowed, scores, negative)
            weights = jnp.exp(scores - jnp.max(scores, axis=-1, keepdims=True))
            probs = weights * (1.0 / jnp.sum(weights, axis=-1, keepdims=True))
            result = jnp.where(mask, dot(probs.astype(jnp.bfloat16), value_rows, 1, 0), result)
        attended_ref[here, :] = result.astype(jnp.bfloat16)


def attend_back_kernel(
    rows, scale,
    qkv_ref, grad_ref, seg_row_ref, seg_col_ref,
    out_ref, sums_ref,
    key_sum, value_sum,
):
    length, part = grad_ref.shape
    masks = head_masks((rows, part))
    key_sum[...] = jnp.zeros_like(key_sum)
    value_sum[...] = jnp.zeros_like(value_sum)
    query_total = jnp.zeros((1, part), jnp.float32)
    for block in range(length // rows):
        here = slice(block * rows, (block + 1) * rows)
        seen = (block + 1) * rows
        queries = qkv_ref[here, :part]
        grads = grad_ref[here, :]
        key_rows = qkv_ref[:seen, part : 2 * part]
        value_rows = qkv_ref[:seen, 2 * part :]
        query_index = block * rows + lax.broadcasted_iota(jnp.int32, (seen, rows), 1)
        key_index = lax.broadcasted_iota(jnp.int32, (seen, rows), 0)
        allowed = (seg_col_ref[:seen, :] == seg_row_ref[:, here]) & (key_index <= query_index)
        grad_query = jnp.zeros((rows, part), jnp.float32)
        for mask in masks:
            head_queries = jnp.where(mask, queries, 0)
            head_grads = jnp.where(mask, grads, 0)
            scores = dot(key_rows, head_queries, 1, 1) * scale
            scores = jnp.where(allowed, scores, negative)
            weights = jnp.exp(scores - jnp.max(scores, axis=0, keepdims=True))
            probs = weights * (1.0 / jnp.sum(weights, axis=0, keepdims=True))
            value_sum[:seen, :] += dot(probs.astype(jnp.bfloat16), head_grads, 1, 0)
            grad_probs = dot(value_rows, head_grads, 1, 1)
            inner = jnp.sum(probs * grad_probs, axis=0, keepdims=True)
            grad_scores = (probs * (grad_probs - inner)).astype(jnp.bfloat16)
            key_sum[:seen, :] += dot(grad_scores, head_queries, 1, 0)
            grad_query = jnp.where(mask, dot(grad_scores, key_rows, 0, 0), grad_query)
        grad_query = (grad_query * scale).astype(jnp.bfloat16)
        out_ref[here, :part] = grad_query
        query_total += jnp.sum(grad_query.astype(jnp.float32), axis=0, keepdims=True)
    grad_values = value_sum[...].astype(jnp.bfloat16)
    out_ref[:, part : 2 * part] = (key_sum[...] * scale).astype(jnp.bfloat16)
    out_ref[:, 2 * part :] = grad_values
    sums_ref[0:1, :] = query_total
    sums_ref[1:2, :] = jnp.sum(grad_values.astype(jnp.float32), axis=0, keepdims=True)


def local(
    tokens,
    segments,
    w_qkv,
    b_qv,
    w_out,
    b_out,
    w_up,
    b_up,
    w_down,
    b_down,
    attngain,
    attnshift,
    mlpgain,
    mlpshift,
    cotangent,
):
    fsdp = lax.axis_size("fsdp")
    owners = fsdp * 2
    ctx_place = lax.axis_index("ctx")
    core_place = lax.axis_index("tp") % 2
    block_len, width = tokens.shape[1:]
    length = segments.shape[1]
    local_width = w_qkv.shape[2]
    part_width = local_width // 2
    part_heads = part_width // HD
    heads_local = local_width // HD
    drow = w_qkv.shape[0]
    hrow = b_qv.shape[2]
    score_scale = 1.0 / HD**0.5

    by_kind = jnp.transpose(w_qkv, (1, 0, 2))
    weight_rows = 3 * drow * part_width // LANES
    own_weight = lax.dynamic_slice_in_dim(by_kind, ctx_place * part_width, part_width, 2)
    sent_weight = lax.dynamic_slice_in_dim(by_kind, (1 - ctx_place) * part_width, part_width, 2)
    small_rows = 32
    up_rows = b_up.shape[0]
    qv_rows = b_qv.shape[0] * b_qv.shape[1]

    def padded(array, first):
        array = array.reshape(-1, array.shape[-1])
        rows, lanes = array.shape
        return jnp.pad(array, ((first, small_rows - first - rows), (0, LANES - lanes)))

    small = padded(b_up, 16) + padded(b_qv, 8)
    for place, vector in enumerate((attngain, attnshift, mlpgain, mlpshift, b_out, b_down)):
        small = small + padded(vector, place)
    out_turned = w_out.T
    small = jnp.concatenate([small, out_turned[:, :part_width], out_turned[:, part_width:]])
    own_pack = jnp.concatenate([own_weight.reshape(weight_rows, LANES), small])
    other_pack = swap(
        jnp.concatenate([sent_weight.reshape(weight_rows, LANES), small]), "ctx"
    )
    own_tokens, w_up, w_down, other_pack = lax.optimization_barrier(
        (tokens[0], w_up, w_down, other_pack)
    )
    half = block_len // 2
    other_block = jnp.concatenate(ordered(core_place, *other_tokens(own_tokens, core_place)))
    all_tokens = jnp.concatenate(ordered(ctx_place, own_tokens, other_block))

    part_hidden = w_up.shape[1] // 2
    own_ffn = jnp.concatenate([w_up, row_major(w_down.T)])
    sent_ffn = lax.dynamic_slice_in_dim(own_ffn, (1 - ctx_place) * part_hidden, part_hidden, 1)
    own_ffn = lax.dynamic_slice_in_dim(own_ffn, ctx_place * part_hidden, part_hidden, 1)
    ffn_pair = jnp.stack(ordered(ctx_place, own_ffn, swap(sent_ffn, "ctx")))
    all_tokens, own_grad = lax.optimization_barrier((all_tokens, cotangent[0]))
    grad_got, grad_turned = other_tokens(own_grad, core_place)

    both_packs = jnp.stack(ordered(ctx_place, own_pack, other_pack))
    packs = gather_fsdp(both_packs)
    packs, ffn_pair = lax.optimization_barrier((packs, ffn_pair))
    up_full = gather_rows(ffn_pair[:, :drow].reshape(-1, part_hidden))
    down_full = gather_rows(ffn_pair[:, drow:].reshape(-1, part_hidden))
    packs = packs.reshape(owners, -1, LANES)
    smalls = packs[:, weight_rows : weight_rows + small_rows].astype(jnp.float32)
    first_vectors = smalls[:, :8, :drow].transpose(1, 0, 2).reshape(8, width)
    qv_bias = (
        smalls[:, 8 : 8 + qv_rows, :hrow].transpose(1, 0, 2).reshape(2, local_width)
    )
    qv_bias_part = lax.dynamic_slice_in_dim(qv_bias, ctx_place * part_width, part_width, 1)
    qkv_bias = jnp.concatenate(
        [qv_bias_part[0], jnp.zeros((part_width,), jnp.float32), qv_bias_part[1]]
    )[None]

    seg_row = segments
    seg_col = segments.reshape(length, 1)
    rows = min(256, length)
    normed_all, qkv_rows, attended_part, qkv_part, out_full = pl.pallas_call(
        functools.partial(attend_kernel, rows, drow, score_scale),
        out_shape=(
            jax.ShapeDtypeStruct((length, width), jnp.bfloat16),
            jax.ShapeDtypeStruct((length, 3 * part_width), jnp.bfloat16),
            jax.ShapeDtypeStruct((length, part_width), jnp.bfloat16),
            jax.ShapeDtypeStruct((width, 3 * part_width), jnp.bfloat16),
            jax.ShapeDtypeStruct((width, local_width), jnp.bfloat16),
        ),
        compiler_params=pltpu.CompilerParams(vmem_limit_bytes=VMEM_LIMIT),
        cost_estimate=pl.CostEstimate(
            flops=2 * length * width * 3 * part_width, bytes_accessed=8 * length * width,
            transcendentals=length * length,
        ),
    )(all_tokens, packs, first_vectors, qkv_bias, seg_row, seg_col)

    def to_tokens(array):
        kept = lax.dynamic_slice_in_dim(array, ctx_place * block_len, block_len, 0)
        sent = swap(
            lax.dynamic_slice_in_dim(array, (1 - ctx_place) * block_len, block_len, 0), "ctx"
        )
        return ordered(ctx_place, kept, sent)

    attended = to_tokens(attended_part)
    attended, up_full, grad_got, grad_turned = lax.optimization_barrier(
        (attended, up_full, grad_got, grad_turned)
    )
    attended = jnp.concatenate(attended, axis=1)
    inputs = own_tokens.astype(jnp.float32)

    def out_part(start, count):
        return dot(lax.dynamic_slice_in_dim(attended, start, count, 0), out_full, 1, 1)

    def small_vectors(gated, unused):
        smalls = gated
        vectors = smalls[:, :8, :drow].transpose(1, 0, 2).reshape(8, width)
        up_bias = lax.dynamic_slice_in_dim(
            smalls[:, 16 : 16 + up_rows, :hrow], ctx_place * (up_rows // 2), up_rows // 2, 1
        )
        up_bias = up_bias.transpose(1, 0, 2).reshape(1, -1)
        return (vectors, up_bias), ()

    attn_sum, (vectors, up_bias_part), unused = sum_tp(
        out_part, block_len, core_place, small_vectors, smalls
    )
    gain_one, shift_one, gain_two, shift_two, out_bias, down_bias = (vectors[i] for i in range(6))
    middle = inputs + (attn_sum.astype(jnp.float32) + out_bias)
    normed_two = normalize(middle, gain_two, shift_two).astype(jnp.bfloat16)
    def hidden(rows):
        return dot(rows, up_full, 1, 0) + up_bias_part

    def hidden_grad(pre, grads):
        grad_activated = dot(grads, down_full, 1, 0)
        value, gelu_pull = jax.vjp(gelu_tanh, pre)
        return gelu_pull(grad_activated)[0].astype(jnp.bfloat16)

    half_rows = lax.dynamic_slice_in_dim(normed_two, core_place * half, half, 0)
    half_rows, late_normed, down_full = lax.optimization_barrier(
        (half_rows, normed_two, down_full)
    )
    got = swap(half_rows, "ctx")
    own_pre = hidden(late_normed)
    own_active = gelu_tanh(own_pre).astype(jnp.bfloat16)
    own_hidden = hidden_grad(own_pre, own_grad)
    other_grad = jnp.concatenate([grad_got, grad_turned])
    got, own_hidden, own_active, other_grad = lax.optimization_barrier(
        (got, own_hidden, own_active, other_grad)
    )
    other_normed = jnp.concatenate([got, swap(got, "tp", CORE)])
    other_pre = hidden(other_normed)
    other_active = gelu_tanh(other_pre).astype(jnp.bfloat16)
    other_hidden = hidden_grad(other_pre, other_grad)

    up_kept, up_sent = chip_parts(own_hidden, other_hidden, up_full, core_place)
    up_sent, own_active, other_active, own_hidden, other_hidden = lax.optimization_barrier(
        (up_sent, own_active, other_active, own_hidden, other_hidden)
    )
    up_got = swap(up_sent, "ctx")
    up_product = (
        dot(normed_two, own_hidden, 0, 0) + dot(other_normed, other_hidden, 0, 0)
    ).astype(jnp.bfloat16)
    mlp_kept, mlp_sent = chip_parts(own_active, other_active, down_full, core_place)
    up_got, up_product, mlp_kept, mlp_sent = lax.optimization_barrier(
        (up_got, up_product, mlp_kept, mlp_sent)
    )
    up_rows_sum = row_major(scatter_rows(up_product))
    up_pair = pair_sum(up_kept, up_got)
    up_pair, own_active, other_active, own_hidden, other_hidden, own_grad, mlp_sent = (
        lax.optimization_barrier(
            (up_pair, own_active, other_active, own_hidden, other_hidden, own_grad, mlp_sent)
        )
    )
    up_across = swap(up_pair, "tp", CHIP)
    mlp_got = swap(mlp_sent, "ctx")
    down_product = (
        dot(own_grad, own_active, 0, 0) + dot(other_grad, other_active, 0, 0)
    ).astype(jnp.bfloat16)
    grad_up_bias = jnp.sum(own_hidden.astype(jnp.float32), axis=0) + jnp.sum(
        other_hidden.astype(jnp.float32), axis=0
    )
    grad_down_bias = jnp.sum(own_grad.astype(jnp.float32), axis=0)
    up_across, mlp_got, down_product, grad_up_bias, grad_down_bias = lax.optimization_barrier(
        (up_across, mlp_got, down_product, grad_up_bias, grad_down_bias)
    )
    down_rows = row_major(scatter_rows(down_product))
    up_total = pair_sum(up_pair, up_across)
    grad_normed_two = jnp.concatenate(
        ordered(core_place, up_total, swap(up_total, "tp", CORE))
    ).astype(jnp.float32)
    grad_out = own_grad.astype(jnp.float32)
    grad_middle_norm, grad_gain_two, grad_shift_two = normalize_back(
        middle, gain_two, grad_normed_two
    )
    grad_middle = grad_out + grad_middle_norm
    grad_branch_low = grad_middle.astype(jnp.bfloat16)
    grad_out_bias = jnp.sum(grad_branch_low.astype(jnp.float32), axis=0)
    grad_attended_low = dot(grad_branch_low, out_full, 1, 0).astype(jnp.bfloat16)
    own_cols = lax.dynamic_slice_in_dim(grad_attended_low, ctx_place * part_width, part_width, 1)
    sent_cols = lax.dynamic_slice_in_dim(
        grad_attended_low, (1 - ctx_place) * part_width, part_width, 1
    )
    sent_cols, late_branch, mlp_got, mlp_kept = lax.optimization_barrier(
        (sent_cols, grad_branch_low, mlp_got, mlp_kept)
    )
    got_cols = swap(sent_cols, "ctx")
    mlp_pair = pair_sum(mlp_kept, mlp_got)
    mlp_across = swap(mlp_pair, "tp", CHIP)
    kept_out, sent_out = weight_product(late_branch, attended, ctx_place)
    got_cols, kept_out, sent_out = lax.optimization_barrier((got_cols, kept_out, sent_out))
    got_out = swap(sent_out, "ctx")
    grad_heads = jnp.concatenate(ordered(ctx_place, own_cols, got_cols))
    grad_qkv_part, bias_sums = pl.pallas_call(
        functools.partial(attend_back_kernel, rows, score_scale),
        out_shape=(
            jax.ShapeDtypeStruct((length, 3 * part_width), jnp.bfloat16),
            jax.ShapeDtypeStruct((2, part_width), jnp.float32),
        ),
        scratch_shapes=[
            pltpu.VMEM((length, part_width), jnp.float32),
            pltpu.VMEM((length, part_width), jnp.float32),
        ],
        compiler_params=pltpu.CompilerParams(vmem_limit_bytes=VMEM_LIMIT),
        cost_estimate=pl.CostEstimate(
            flops=10 * length * length * part_width, bytes_accessed=2 * length * width,
            transcendentals=length * length,
        ),
    )(qkv_rows, grad_heads, seg_row, seg_col)
    def token_rows(ctx, core):
        return lax.dynamic_slice_in_dim(grad_qkv_part, (2 * ctx + core) * half, half, 0)

    first_sent = chip_sum_rows(
        token_rows(1 - ctx_place, 1 - core_place), token_rows(1 - ctx_place, core_place), qkv_part
    )
    first_kept = chip_sum_rows(
        token_rows(ctx_place, 1 - core_place), token_rows(ctx_place, core_place), qkv_part
    )
    first_sent, late_part = lax.optimization_barrier((first_sent, grad_qkv_part))
    first_got = swap(first_sent, "ctx")
    grad_qkv_weight = dot(normed_all, late_part, 0, 0).astype(jnp.bfloat16)
    first_got, first_kept, grad_qkv_weight, kept_out, got_out, mlp_across, mlp_pair = (
        lax.optimization_barrier(
            (first_got, first_kept, grad_qkv_weight, kept_out, got_out, mlp_across, mlp_pair)
        )
    )
    grad_qkv_sum = row_major(scatter_rows(grad_qkv_weight)).astype(jnp.float32)
    own_rows = lax.dynamic_slice_in_dim(grad_qkv_sum, ctx_place * drow, drow, 0)
    sent_rows = swap(
        lax.dynamic_slice_in_dim(grad_qkv_sum, (1 - ctx_place) * drow, drow, 0).astype(
            jnp.bfloat16
        ),
        "ctx",
    ).astype(jnp.float32)
    grad_qkv_out = jnp.concatenate(
        [
            part.reshape(drow, 3, part_width)
            for part in ordered(ctx_place, own_rows, sent_rows)
        ],
        axis=2,
    )
    nothing = jnp.zeros_like(bias_sums)
    grad_qv_bias = jnp.concatenate(ordered(ctx_place, bias_sums, nothing), axis=1)

    def by_owner(vector):
        return vector.reshape(owners, 1, drow)

    def row_block(array, first):
        rows, lanes = array.shape[1:]
        return jnp.pad(
            array, ((0, 0), (first, small_rows - first - rows), (0, LANES - lanes))
        )

    def small_work(gated, chip_sum):
        up_rows_sum, down_rows, grad_up_bias, mlp_pair, mlp_across, kept_out, got_out = gated
        ffn_rows = jnp.stack([up_rows_sum, down_rows]).reshape(2, 2, drow, part_hidden)
        ffn_kept, ffn_sent = ordered(ctx_place, ffn_rows[:, 0], ffn_rows[:, 1])
        ffn_got = swap(ffn_sent, "ctx")
        half_inputs = lax.dynamic_slice_in_dim(inputs, core_place * half, half, 0)
        half_grad = chip_sum.astype(jnp.float32)
        unused, gain_share, shift_share = normalize_back(half_inputs, gain_one, half_grad)
        up_bias_rows = grad_up_bias.reshape(up_rows // 2, HD)
        up_bias_rows = jnp.concatenate(
            ordered(ctx_place, up_bias_rows, jnp.zeros_like(up_bias_rows))
        )
        small_grads = row_block(
            up_bias_rows.reshape(up_rows, owners, hrow).transpose(1, 0, 2), 16
        ) + row_block(grad_qv_bias.reshape(qv_rows, owners, hrow).transpose(1, 0, 2), 8)
        for place, vector in enumerate(
            (
                gain_share,
                shift_share,
                grad_gain_two,
                grad_shift_two,
                grad_out_bias,
                grad_down_bias,
            )
        ):
            small_grads = small_grads + row_block(by_owner(vector), place)
        small_sums = jnp.sum(
            lax.all_to_all(small_grads, ("fsdp", "ctx"), 0, 0, tiled=True), axis=0
        )
        mlp_total = pair_sum(mlp_pair, mlp_across)
        return (small_sums, ffn_kept, mlp_total, pair_sum(kept_out, got_out)), ffn_got

    first_pair = pair_sum(first_kept, first_got)
    first_pair, gated = lax.optimization_barrier(
        (
            first_pair,
            (up_rows_sum, down_rows, grad_up_bias, mlp_pair, mlp_across, kept_out, got_out),
        )
    )
    first_across = swap(first_pair, "tp", CHIP)
    done, ffn_got = small_work(gated, first_pair)
    first_across, done = lax.optimization_barrier((first_across, done))
    small_sums, ffn_kept, mlp_total, out_pairs = done
    grad_out_weight = row_major(scatter_rows(out_pairs))
    first_total = pair_sum(first_pair, first_across)
    first_sum = jnp.concatenate(
        ordered(core_place, first_total, swap(first_total, "tp", CORE))
    )
    grad_up, grad_down = jnp.concatenate(ordered(ctx_place, ffn_kept, ffn_got), axis=2)
    mlp_sum = jnp.concatenate(ordered(core_place, mlp_total, swap(mlp_total, "tp", CORE)))
    finished = middle + (mlp_sum.astype(jnp.float32) + down_bias)
    grad_inputs_norm, unused, unused = normalize_back(
        inputs, gain_one, first_sum.astype(jnp.float32)
    )
    grad_inputs = grad_middle + grad_inputs_norm
    share = small_sums[:2]
    share = share + swap(share, "tp", CORE)
    share = share + swap(share, "tp", CHIP)
    gain_one_sum, shift_one_sum = share[0, :drow], share[1, :drow]
    vector_sums = small_sums[:8, :drow]
    up_bias_sum = small_sums[16 : 16 + up_rows, :hrow]
    qv_bias_sum = small_sums[8 : 8 + qv_rows, :hrow].reshape(2, heads_local, hrow)

    return (
        finished.astype(jnp.bfloat16)[None],
        grad_inputs[None],
        grad_qkv_out,
        qv_bias_sum,
        grad_out_weight.T.astype(jnp.float32),
        vector_sums[4],
        grad_up.astype(jnp.float32),
        up_bias_sum,
        grad_down.T.astype(jnp.float32),
        vector_sums[5],
        gain_one_sum,
        shift_one_sum,
        vector_sums[2],
        vector_sums[3],
    )


def solution(mesh):
    placed = (
        P("fsdp", "ctx", None),
        P("fsdp", None),
        P(("fsdp", "ctx"), None, "tp"),
        P(None, "tp", ("fsdp", "ctx")),
        P("tp", ("fsdp", "ctx")),
        P(("fsdp", "ctx")),
        P(("fsdp", "ctx"), "tp"),
        P("tp", ("fsdp", "ctx")),
        P("tp", ("fsdp", "ctx")),
        P(("fsdp", "ctx")),
        P(("fsdp", "ctx")),
        P(("fsdp", "ctx")),
        P(("fsdp", "ctx")),
        P(("fsdp", "ctx")),
        P("fsdp", "ctx", None),
    )
    return jax.shard_map(
        local,
        mesh=mesh,
        in_specs=placed,
        out_specs=(
            P("fsdp", "ctx", None),
            P("fsdp", "ctx", None),
            P(("fsdp", "ctx"), None, "tp"),
            P(None, "tp", ("fsdp", "ctx")),
            P("tp", ("fsdp", "ctx")),
            P(("fsdp", "ctx")),
            P(("fsdp", "ctx"), "tp"),
            P("tp", ("fsdp", "ctx")),
            P("tp", ("fsdp", "ctx")),
            P(("fsdp", "ctx")),
            P(("fsdp", "ctx")),
            P(("fsdp", "ctx")),
            P(("fsdp", "ctx")),
            P(("fsdp", "ctx")),
        ),
        check_vma=False,
    )
```

profile of v0, /device:TPU:0, one launch (start us, length us, event | category | flops | bytes accessed | tf_op | source)
XLA Modules:
  0.0 304.6 jit_solution(15187420865757956078)
XLA Ops:
  10.8 3.0 collective-permute-start
  13.8 4.4 %collective-permute-done = bf16[672,128]{1,0:T(8,128)(2,1)S(1)} collective-permute-done((bf16[672,128]{1,0:T(8,128)(2,1)S(1)}, bf16[672,128]{1,0:T(8,128)(2,1)S(1)}, u32[]{:S(2)}, u32[]{:S(2)}) %collective-permute-start) | collective-permute-done | bytes 172064 | tf_op jit(solution)/shard_map/ppermute | solution.py:23
  19.2 1.8 collective-permute-start.1
  22.4 4.9 %all-to-all-start = ((bf16[4,2,672,128]{3,2,1,0:T(8,128)(2,1)}), bf16[4,2,672,128]{3,2,1,0:T(8,128)(2,1)}, u32[]{:S(2)}, u32[]{:S(2)}) async-start(bf16[4,2,672,128]{3,2,1,0:T(8,128)(2,1)} %broadcast_in_dim.14), calls=%async_computation | async-start | bytes 2752512 | tf_op jit(solution)/shard_map/all_to_all | solution.py:32
  27.3 5.1 %collective-permute-done.1 = bf16[256,1024]{1,0:T(8,128)(2,1)S(1)} collective-permute-done((bf16[256,1024]{1,0:T(8,128)(2,1)S(1)}, bf16[256,1024]{1,0:T(8,128)(2,1)S(1)}, u32[]{:S(2)}, u32[]{:S(2)}) %collective-permute-start.1) | collective-permute-done | bytes 524320 | tf_op jit(solution)/shard_map/ppermute | solution.py:23
  33.3 1.4 collective-permute-start.3
  34.8 1.9 broadcast_select_fusion.1
  40.0 2.7 collective-permute-done.3
  43.9 9.6 %collective-permute-done.5 = bf16[256,1024]{1,0:T(8,128)(2,1)} collective-permute-done((bf16[256,1024]{1,0:T(8,128)(2,1)}, bf16[256,1024]{1,0:T(8,128)(2,1)}, u32[]{:S(2)}, u32[]{:S(2)}) %collective-permute-start.5) | collective-permute-done | bytes 524320 | tf_op jit(solution)/shard_map/ppermute | solution.py:23
  53.6 5.5 %all-to-all-done = bf16[4,2,672,128]{3,2,1,0:T(8,128)(2,1)} async-done(((bf16[4,2,672,128]{3,2,1,0:T(8,128)(2,1)}), bf16[4,2,672,128]{3,2,1,0:T(8,128)(2,1)}, u32[]{:S(2)}, u32[]{:S(2)}) %all-to-all-start) | async-done | bytes 1376288 | tf_op jit(solution)/shard_map/all_to_all | solution.py:32
  61.0 7.7 %shard_map.254 = (bf16[1024,1024]{1,0:T(8,128)(2,1)S(1)}, bf16[1024,384]{1,0:T(8,128)(2,1)S(1)}, bf16[1024,128]{1,0:T(8,128)(2,1)S(1)}, bf16[1024,384]{1,0:T(8,128)(2,1)S(1)}, bf16[1024,256]{1,0:T(8,128)(2,1)S(1)}) custom-call(bf16[1024,1024]{1,0:T(8,128)(2,1)S(1)} %pad_maximum_fusion.tokens_ref, bf16[8,672,128]{2,1,0:T(8,128)(2,1)} %bitcast.19.packs_ref, ...), custom_call_target="tpu_custom_call" | custom-call | flops 805306368 | bytes 8388608 | tf_op jit(solution)/shard_map/pallas_call | solution.py:314
  69.5 1.3 copy-done.4
  73.0 4.5 %collective-permute-done.4 = bf16[512,128]{1,0:T(8,128)(2,1)S(1)} collective-permute-done((bf16[512,128]{1,0:T(8,128)(2,1)S(1)}, bf16[512,128]{1,0:T(8,128)(2,1)S(1)}, u32[]{:S(2)}, u32[]{:S(2)}) %collective-permute-start.4) | collective-permute-done | bytes 131104 | tf_op jit(solution)/shard_map/ppermute | solution.py:23
  78.4 7.7 %all-gather.3.cloned.1.call-done = bf16[1024,512]{1,0:T(8,128)(2,1)} async-done(((bf16[256,512]{1,0:T(8,128)(2,1)}), bf16[1024,512]{1,0:T(8,128)(2,1)}) %all-gather.3.cloned.1.call-update) | async-done | bytes 1048592 | tf_op jit(solution)/shard_map/all_gather | solution.py:38
  86.2 1.4 convolution_convert_fusion.8
  87.7 1.9 collective-permute-done.7
  89.9 1.5 collective-permute-start.8
  92.2 11.8 %collective-permute-done.8 = bf16[256,1024]{1,0:T(8,128)(2,1)S(1)} collective-permute-done((bf16[256,1024]{1,0:T(8,128)(2,1)S(1)}, bf16[256,1024]{1,0:T(8,128)(2,1)S(1)}, u32[]{:S(2)}, u32[]{:S(2)}) %collective-permute-start.8) | collective-permute-done | bytes 524320 | tf_op jit(solution)/shard_map/ppermute | solution.py:23
  105.3 2.2 pad_maximum_fusion.2
  113.0 19.7 %all-gather.5.cloned.1.call-done = bf16[1024,512]{1,0:T(8,128)(2,1)} async-done(((bf16[256,512]{1,0:T(8,128)(2,1)}), bf16[1024,512]{1,0:T(8,128)(2,1)}) %all-gather.5.cloned.1.call-update) | async-done | bytes 1048592 | tf_op jit(solution)/shard_map/all_gather | solution.py:38
  132.7 1.5 collective-permute-start.10
  134.2 2.2 fusion.78
  136.5 2.5 multiply_convert_fusion.1
  139.0 7.5 %collective-permute-done.10 = bf16[256,1024]{1,0:T(8,128)(2,1)S(1)} collective-permute-done((bf16[256,1024]{1,0:T(8,128)(2,1)}, bf16[256,1024]{1,0:T(8,128)(2,1)S(1)}, u32[]{:S(2)}, u32[]{:S(2)}) %collective-permute-start.10) | collective-permute-done | bytes 524320 | tf_op jit(solution)/shard_map/ppermute | solution.py:23
  148.4 2.3 multiply_convert_fusion
  152.1 1.5 dynamic-slice_reduce_fusion
  153.6 2.7 convolution_convert_fusion.7
  156.7 2.3 fusion.9
  159.0 1.5 collective-permute-start.14
  160.5 1.3 convolution_convert_fusion.5
  161.8 1.3 convolution_convert_fusion.4
  164.4 1.7 add_convert_fusion.2
  166.1 2.8 add_convert_fusion.11
  168.9 2.4 add_convert_fusion.10
  171.3 2.0 collective-permute-done.14
  173.4 3.0 fusion.12
  176.4 1.5 collective-permute-start.17
  177.9 1.5 collective-permute-start.18
  179.4 1.8 fusion.81
  181.6 1.7 add_convert_fusion.1
  183.3 6.6 %collective-permute-done.17 = bf16[256,1024]{1,0:T(8,128)(2,1)} collective-permute-done((bf16[256,1024]{1,0:T(8,128)(2,1)}, bf16[256,1024]{1,0:T(8,128)(2,1)}, u32[]{:S(2)}, u32[]{:S(2)}) %collective-permute-start.17) | collective-permute-done | bytes 524320 | tf_op jit(solution)/shard_map/ppermute | solution.py:23
  191.1 2.2 add_convert_fusion.9
  193.3 1.5 multiply_reduce_fusion.3
  196.9 2.6 fusion.6
  199.5 11.0 %convert_reduce_fusion.2 = (f32[1024]{0:T(1024)S(1)}, bf16[512,1024]{1,0:T(8,128)(2,1)S(1)}, f32[512,1024]{1,0:T(8,128)}) fusion(f32[512]{0:T(512)S(1)} %broadcast_multiply_fusion.3, f32[512]{0:T(512)S(1)} %broadcast_multiply_fusion.5, f32[1024]{0:T(1024)S(1)} %bitcast.185, bf16[256,1024]{1,0:T(8,128)(2,1)S(1)} %copy-done.13, ...), kind=kLoop, calls=%fused_computation.19 | loop fusion | flops 12057600 | bytes 7360512 | tf_op jit(solution)/shard_map/reduce_sum | solution.py:429
  211.1 1.5 collective-permute-start.20
  213.1 2.1 add_convert_fusion.6
  216.7 7.0 %shard_map.255 = (bf16[1024,384]{1,0:T(8,128)(2,1)S(1)}, f32[2,128]{1,0:T(2,128)S(1)}) custom-call(bf16[1024,384]{1,0:T(8,128)(2,1)S(1)} %copy-done.6, bf16[1024,128]{1,0:T(8,128)(2,1)S(1)} %pad_maximum_fusion.10.grad_ref, s32[1,1024]{1,0:T(1,128)S(1)} %copy-done.3, s32[1024,1]{1,0:T(8,128)S(1)} %copy.91.seg_col_ref), custom_call_target="tpu_custom_call" | custom-call | flops 1342177280 | bytes 2097152 | tf_op jit(solution)/shard_map/pallas_call | solution.py:445
  226.8 1.5 collective-permute-start.24
  228.4 2.3 add_convert_fusion.8
  231.3 3.8 %convolution_convert_fusion = bf16[1024,384]{1,0:T(8,128)(2,1)} fusion(bf16[1024,1024]{1,0:T(8,128)(2,1)} %copy-done.4, bf16[1024,384]{1,0:T(8,128)(2,1)S(1)} %get-tuple-element.148), kind=kOutput, calls=%fused_computation.38 | convolution fusion | flops 805699584 | bytes 3670016 | tf_op jit(solution)/shard_map/dot_general | solution.py:126
  236.3 10.3 %collective-permute-done.22 = bf16[256,1024]{1,0:T(8,128)(2,1)} collective-permute-done((bf16[256,1024]{1,0:T(8,128)(2,1)}, bf16[256,1024]{1,0:T(8,128)(2,1)}, u32[]{:S(2)}, u32[]{:S(2)}) %collective-permute-start.22) | collective-permute-done | bytes 524320 | tf_op jit(solution)/shard_map/ppermute | solution.py:23
  246.6 2.0 add_convert_fusion.5
  248.7 1.4 collective-permute-start.26
  250.1 1.3 fusion.25
  252.4 3.5 %all-to-all-start.1 = ((f32[8,32,128]{2,1,0:T(8,128)}), f32[8,32,128]{2,1,0:T(8,128)S(1)}, u32[]{:S(2)}, u32[]{:S(2)}) async-start(f32[8,32,128]{2,1,0:T(8,128)} %copy.96), calls=%async_computation.3 | async-start | bytes 262144 | tf_op jit(solution)/shard_map/all_to_all | solution.py:532
  256.2 1.3 select_bitcast_fusion
  257.5 2.1 collective-permute-start.30
  259.6 1.4 add_convert_fusion.4
  261.0 1.7 add_convert_fusion.14
  262.7 3.3 %all-to-all-done.1 = f32[8,32,128]{2,1,0:T(8,128)S(1)} async-done(((f32[8,32,128]{2,1,0:T(8,128)}), f32[8,32,128]{2,1,0:T(8,128)S(1)}, u32[]{:S(2)}, u32[]{:S(2)}) %all-to-all-start.1) | async-done | bytes 131104 | tf_op jit(solution)/shard_map/all_to_all | solution.py:532
  269.4 1.5 collective-permute-start.32
  277.9 3.3 %add_bitcast_fusion = (f32[1,512,1024]{2,1,0:T(8,128)}, bf16[1,512,1024]{2,1,0:T(8,128)(2,1)}) fusion(f32[512,1024]{1,0:T(8,128)S(1)} %copy-done.24, bf16[512,1024]{1,0:T(8,128)(2,1)S(1)} %bitcast.163, f32[512]{0:T(512)S(1)} %broadcast_multiply_fusion, f32[512]{0:T(512)S(1)} %broadcast_multiply_fusion.1, f32[1024]{0:T(1024)S(1)} %bitcast.193, ...), kind=kLoop, calls=%fused_computation.13 | loop fusion | flops 13631488 | bytes 9457664 | tf_op jit(solution)/shard_map/broadcast_in_dim | solution.py:570
  283.4 11.2 %reduce-scatter.11.cloned.1.call-done = bf16[128,256]{1,0:T(8,128)(2,1)} async-done(((bf16[512,256]{1,0:T(8,128)(2,1)}), bf16[128,256]{1,0:T(8,128)(2,1)}) %reduce-scatter.11.cloned.1.call-update) | async-done | bytes 65552 | tf_op jit(solution)/shard_map/reduce_scatter | solution.py:97
  (255 shorter events, 57.8 us)
Async XLA Ops:
  10.8 7.4 %collective-permute-start = (bf16[672,128]{1,0:T(8,128)(2,1)S(1)}, bf16[672,128]{1,0:T(8,128)(2,1)S(1)}, u32[]{:S(2)}, u32[]{:S(2)}) collective-permute-start(bf16[672,128]{1,0:T(8,128)(2,1)S(1)} %pad_maximum_fusion.14), channel_id=1, source_target_pairs={{0,4},{4,0},{1,5},{5,1},{2,6},{6,2},{3,7},{7,3},{8,12},{12,8},{9,1... | collective-permute-start | bytes 516104 | tf_op jit(solution)/shard_map/ppermute | solution.py:23
  19.2 13.2 %collective-permute-start.1 = (bf16[256,1024]{1,0:T(8,128)(2,1)S(1)}, bf16[256,1024]{1,0:T(8,128)(2,1)S(1)}, u32[]{:S(2)}, u32[]{:S(2)}) collective-permute-start(bf16[256,1024]{1,0:T(8,128)(2,1)S(1)} %constant_dynamic-slice_fusion.6), channel_id=1, source_target_pairs={{0,4},{4,0},{1,5},{5,1},{2,6},{6,2},{3,7},{7,3},{8,12},{12,8},{9,1... | collective-permute-start | bytes 1572872 | tf_op jit(solution)/shard_map/ppermute | solution.py:23
  21.1 11.3 %copy-start.43 = (bf16[1024,128]{1,0:T(8,128)(2,1)S(1)}, bf16[1024,128]{1,0:T(8,128)(2,1)}, u32[]{:S(2)}) copy-start(bf16[1024,128]{1,0:T(8,128)(2,1)} %param.23) | copy-start | bytes 786436
  21.2 11.4 %copy-start.42 = (bf16[128,1024]{1,0:T(8,128)(2,1)S(1)}, bf16[128,1024]{1,0:T(8,128)(2,1)}, u32[]{:S(2)}) copy-start(bf16[128,1024]{1,0:T(8,128)(2,1)} %param.21) | copy-start | bytes 786436
  22.4 36.6 %all-to-all-start = ((bf16[4,2,672,128]{3,2,1,0:T(8,128)(2,1)}), bf16[4,2,672,128]{3,2,1,0:T(8,128)(2,1)}, u32[]{:S(2)}, u32[]{:S(2)}) async-start(bf16[4,2,672,128]{3,2,1,0:T(8,128)(2,1)} %broadcast_in_dim.14), calls=%async_computation | async-start | bytes 2752512 | tf_op jit(solution)/shard_map/all_to_all | solution.py:32
  27.3 7.5 %copy-start.7 = (bf16[1,512,1024]{2,1,0:T(8,128)(2,1)S(1)}, bf16[1,512,1024]{2,1,0:T(8,128)(2,1)}, u32[]{:S(2)}) copy-start(bf16[1,512,1024]{2,1,0:T(8,128)(2,1)} %param.15) | copy-start | bytes 3145732
  27.3 58.8 %all-gather.3.cloned.1.call-start = ((), (), s32[]{:S(2)}) async-start(), calls=%async_computation.6 | async-start | bytes 1310720 | tf_op jit(solution)/shard_map/all_gather | solution.py:38
  32.4 2.3 collective-permute-start.2
  33.3 9.4 %collective-permute-start.3 = (bf16[256,512]{1,0:T(8,128)(2,1)}, bf16[256,512]{1,0:T(8,128)(2,1)}, u32[]{:S(2)}, u32[]{:S(2)}) collective-permute-start(bf16[256,512]{1,0:T(8,128)(2,1)} %fusion.32), channel_id=1, source_target_pairs={{0,4},{4,0},{1,5},{5,1},{2,6},{6,2},{3,7},{7,3},{8,12},{12,8},{9,1... | collective-permute-start | bytes 786440 | tf_op jit(solution)/shard_map/ppermute | solution.py:23
  38.8 14.8 %collective-permute-start.5 = (bf16[256,1024]{1,0:T(8,128)(2,1)}, bf16[256,1024]{1,0:T(8,128)(2,1)}, u32[]{:S(2)}, u32[]{:S(2)}) collective-permute-start(bf16[256,1024]{1,0:T(8,128)(2,1)} %constant_dynamic-slice_fusion.2), channel_id=1, source_target_pairs={{0,4},{4,0},{1,5},{5,1},{2,6},{6,2},{3,7},{7,3},{8,12},{12,8},{9,1... | collective-permute-start | bytes 1572872 | tf_op jit(solution)/shard_map/ppermute | solution.py:23
  53.6 24.9 %collective-permute-start.6 = (bf16[256,1024]{1,0:T(8,128)(2,1)}, bf16[256,1024]{1,0:T(8,128)(2,1)}, u32[]{:S(2)}, u32[]{:S(2)}) collective-permute-start(bf16[256,1024]{1,0:T(8,128)(2,1)} %collective-permute-done.5), channel_id=1, source_target_pairs={{0,1},{1,0},{2,3},{3,2},{4,5},{5,4},{6,7},{7,6},{8,9},{9,8},{10,11... | collective-permute-start | bytes 1572872 | tf_op jit(solution)/shard_map/ppermute | solution.py:23
  59.9 72.8 %all-gather.5.cloned.1.call-start = ((), (), s32[]{:S(2)}) async-start(), calls=%async_computation.7 | async-start | bytes 1310720 | tf_op jit(solution)/shard_map/all_gather | solution.py:38
  72.4 17.2 %copy-start.1 = (bf16[1024,256]{1,0:T(8,128)(2,1)S(1)}, bf16[1024,256]{1,0:T(8,128)(2,1)}, u32[]{:S(2)}) copy-start(bf16[1024,256]{1,0:T(8,128)(2,1)} %copy-done) | copy-start | bytes 1572868
  72.4 5.0 %collective-permute-start.4 = (bf16[512,128]{1,0:T(8,128)(2,1)S(1)}, bf16[512,128]{1,0:T(8,128)(2,1)S(1)}, u32[]{:S(2)}, u32[]{:S(2)}) collective-permute-start(bf16[512,128]{1,0:T(8,128)(2,1)S(1)} %constant_dynamic-slice_fusion.3), channel_id=1, source_target_pairs={{0,4},{4,0},{1,5},{5,1},{2,6},{6,2},{3,7},{7,3},{8,12},{12,8},{9,1... | collective-permute-start | bytes 393224 | tf_op jit(solution)/shard_map/ppermute | solution.py:23
  87.6 2.0 collective-permute-start.7
  89.9 14.0 %collective-permute-start.8 = (bf16[256,1024]{1,0:T(8,128)(2,1)S(1)}, bf16[256,1024]{1,0:T(8,128)(2,1)S(1)}, u32[]{:S(2)}, u32[]{:S(2)}) collective-permute-start(bf16[256,1024]{1,0:T(8,128)(2,1)S(1)} %add_convert_fusion.13), channel_id=1, source_target_pairs={{0,2},{1,3},{2,0},{3,1},{4,6},{5,7},{6,4},{7,5},{8,10},{9,11},{10,... | collective-permute-start | bytes 1572872 | tf_op jit(solution)/shard_map/ppermute | solution.py:23
  92.2 15.3 %copy-start.44 = (f32[8,1024]{1,0:T(8,128)S(1)}, f32[8,1024]{1,0:T(8,128)}, u32[]{:S(2)}) copy-start(f32[8,1024]{1,0:T(8,128)} %slice_bitcast_fusion.4) | copy-start | bytes 98308
  104.9 2.6 collective-permute-start.9
  105.0 3.9 %copy-start.8 = (bf16[1,512,1024]{2,1,0:T(8,128)(2,1)S(1)}, bf16[1,512,1024]{2,1,0:T(8,128)(2,1)}, u32[]{:S(2)}) copy-start(bf16[1,512,1024]{2,1,0:T(8,128)(2,1)} %param.15) | copy-start | bytes 3145732
  105.0 143.7 %reduce-scatter.5.cloned.1.call-start = ((), (), s32[]{:S(2)}) async-start(), calls=%async_computation.8 | async-start | bytes 1310720 | tf_op jit(solution)/shard_map/reduce_scatter | solution.py:97
  132.7 3.7 %copy-start.26 = (bf16[512,1024]{1,0:T(8,128)(2,1)S(1)}, bf16[512,1024]{1,0:T(8,128)(2,1)}, u32[]{:S(2)}) copy-start(bf16[512,1024]{1,0:T(8,128)(2,1)} %copy-done.25) | copy-start | bytes 3145732
  132.7 13.7 %collective-permute-start.10 = (bf16[256,1024]{1,0:T(8,128)(2,1)}, bf16[256,1024]{1,0:T(8,128)(2,1)S(1)}, u32[]{:S(2)}, u32[]{:S(2)}) collective-permute-start(bf16[256,1024]{1,0:T(8,128)(2,1)} %constant_dynamic-slice_fusion.1), channel_id=1, source_target_pairs={{0,4},{4,0},{1,5},{5,1},{2,6},{6,2},{3,7},{7,3},{8,12},{12,8},{9,1... | collective-permute-start | bytes 1572872 | tf_op jit(solution)/shard_map/ppermute | solution.py:23
  136.4 10.0 %copy-start.17 = (bf16[1024,512]{1,0:T(8,128)(2,1)S(1)}, bf16[1024,512]{1,0:T(8,128)(2,1)}, u32[]{:S(2)}) copy-start(bf16[1024,512]{1,0:T(8,128)(2,1)} %all-gather.5.cloned.1.call-done) | copy-start | bytes 3145732
  136.4 10.0 %copy-start.34 = (bf16[512,1024]{1,0:T(8,128)(2,1)S(1)}, bf16[512,1024]{1,0:T(8,128)(2,1)}, u32[]{:S(2)}) copy-start(bf16[512,1024]{1,0:T(8,128)(2,1)} %pad_maximum_fusion.2) | copy-start | bytes 3145732
  146.4 1.9 collective-permute-start.12
  151.9 4.7 %collective-permute-start.13 = (bf16[256,1024]{1,0:T(8,128)(2,1)}, bf16[256,1024]{1,0:T(8,128)(2,1)}, u32[]{:S(2)}, u32[]{:S(2)}) collective-permute-start(bf16[256,1024]{1,0:T(8,128)(2,1)} %convolution_convert_fusion.6), channel_id=1, source_target_pairs={{0,1},{1,0},{2,3},{3,2},{4,5},{5,4},{6,7},{7,6},{8,9},{9,8},{10,11... | collective-permute-start | bytes 1572872 | tf_op jit(solution)/shard_map/ppermute | solution.py:23
  152.1 4.6 %copy-start.16 = (bf16[1024,512]{1,0:T(8,128)(2,1)S(1)}, bf16[1024,512]{1,0:T(8,128)(2,1)}, u32[]{:S(2)}) copy-start(bf16[1024,512]{1,0:T(8,128)(2,1)} %all-gather.3.cloned.1.call-done) | copy-start | bytes 3145732
  152.1 4.6 %copy-start.30 = (bf16[512,512]{1,0:T(8,128)(2,1)S(1)}, bf16[512,512]{1,0:T(8,128)(2,1)}, u32[]{:S(2)}) copy-start(bf16[512,512]{1,0:T(8,128)(2,1)} %copy-done.29) | copy-start | bytes 1572868
  153.6 6.9 %copy-start.18 = (bf16[1024,512]{1,0:T(8,128)(2,1)S(1)}, bf16[1024,512]{1,0:T(8,128)(2,1)}, u32[]{:S(2)}) copy-start(bf16[1024,512]{1,0:T(8,128)(2,1)} %all-gather.5.cloned.1.call-done) | copy-start | bytes 3145732
  153.6 6.9 %copy-start.41 = (bf16[512,512]{1,0:T(8,128)(2,1)S(1)}, bf16[512,512]{1,0:T(8,128)(2,1)}, u32[]{:S(2)}) copy-start(bf16[512,512]{1,0:T(8,128)(2,1)} %get-tuple-element.134) | copy-start | bytes 1572868
  156.3 5.5 %copy-start.38 = (bf16[512,512]{1,0:T(8,128)(2,1)S(1)}, bf16[512,512]{1,0:T(8,128)(2,1)}, u32[]{:S(2)}) copy-start(bf16[512,512]{1,0:T(8,128)(2,1)} %get-tuple-element.135) | copy-start | bytes 1572868
  156.3 17.1 %collective-permute-start.11 = (bf16[256,1024]{1,0:T(8,128)(2,1)}, bf16[256,1024]{1,0:T(8,128)(2,1)}, u32[]{:S(2)}, u32[]{:S(2)}) collective-permute-start(bf16[256,1024]{1,0:T(8,128)(2,1)} %convolution_convert_fusion.7), channel_id=1, source_target_pairs={{0,1},{1,0},{2,3},{3,2},{4,5},{5,4},{6,7},{7,6},{8,9},{9,8},{10,11... | collective-permute-start | bytes 1572872 | tf_op jit(solution)/shard_map/ppermute | solution.py:23
  159.0 4.6 %copy-start.27 = (bf16[512,1024]{1,0:T(8,128)(2,1)S(1)}, bf16[512,1024]{1,0:T(8,128)(2,1)}, u32[]{:S(2)}) copy-start(bf16[512,1024]{1,0:T(8,128)(2,1)} %copy-done.25) | copy-start | bytes 3145732
  159.0 4.6 %copy-start.32 = (bf16[512,512]{1,0:T(8,128)(2,1)S(1)}, bf16[512,512]{1,0:T(8,128)(2,1)}, u32[]{:S(2)}) copy-start(bf16[512,512]{1,0:T(8,128)(2,1)} %get-tuple-element.136) | copy-start | bytes 1572868
  159.0 14.3 %collective-permute-start.14 = (bf16[256,1024]{1,0:T(8,128)(2,1)}, bf16[256,1024]{1,0:T(8,128)(2,1)}, u32[]{:S(2)}, u32[]{:S(2)}) collective-permute-start(bf16[256,1024]{1,0:T(8,128)(2,1)} %fusion.9), channel_id=1, source_target_pairs={{0,4},{4,0},{1,5},{5,1},{2,6},{6,2},{3,7},{7,3},{8,12},{12,8},{9,1... | collective-permute-start | bytes 1572872 | tf_op jit(solution)/shard_map/ppermute | solution.py:23
  161.7 4.4 %collective-permute-start.15 = (bf16[256,1024]{1,0:T(8,128)(2,1)}, bf16[256,1024]{1,0:T(8,128)(2,1)}, u32[]{:S(2)}, u32[]{:S(2)}) collective-permute-start(bf16[256,1024]{1,0:T(8,128)(2,1)} %convolution_convert_fusion.5), channel_id=1, source_target_pairs={{0,1},{1,0},{2,3},{3,2},{4,5},{5,4},{6,7},{7,6},{8,9},{9,8},{10,11... | collective-permute-start | bytes 1572872 | tf_op jit(solution)/shard_map/ppermute | solution.py:23
  163.1 5.8 %collective-permute-start.16 = (bf16[256,1024]{1,0:T(8,128)(2,1)}, bf16[256,1024]{1,0:T(8,128)(2,1)}, u32[]{:S(2)}, u32[]{:S(2)}) collective-permute-start(bf16[256,1024]{1,0:T(8,128)(2,1)} %convolution_convert_fusion.4), channel_id=1, source_target_pairs={{0,1},{1,0},{2,3},{3,2},{4,5},{5,4},{6,7},{7,6},{8,9},{9,8},{10,11... | collective-permute-start | bytes 1572872 | tf_op jit(solution)/shard_map/ppermute | solution.py:23
  173.3 75.3 %reduce-scatter.7.cloned.1.call-start = ((), (), s32[]{:S(2)}) async-start(), calls=%async_computation.9 | async-start | bytes 1310720 | tf_op jit(solution)/shard_map/reduce_scatter | solution.py:97
  173.4 6.0 %copy-start.22 = (bf16[1,512,1024]{2,1,0:T(8,128)(2,1)S(1)}, bf16[1,512,1024]{2,1,0:T(8,128)(2,1)}, u32[]{:S(2)}) copy-start(bf16[1,512,1024]{2,1,0:T(8,128)(2,1)} %param.29) | copy-start | bytes 3145732
  176.4 4.8 %copy-start.31 = (bf16[512,512]{1,0:T(8,128)(2,1)S(1)}, bf16[512,512]{1,0:T(8,128)(2,1)}, u32[]{:S(2)}) copy-start(bf16[512,512]{1,0:T(8,128)(2,1)} %copy-done.29) | copy-start | bytes 1572868
  176.4 4.8 %copy-start.33 = (bf16[512,512]{1,0:T(8,128)(2,1)S(1)}, bf16[512,512]{1,0:T(8,128)(2,1)}, u32[]{:S(2)}) copy-start(bf16[512,512]{1,0:T(8,128)(2,1)} %get-tuple-element.136) | copy-start | bytes 1572868
  176.4 5.2 %copy-start.35 = (bf16[512,1024]{1,0:T(8,128)(2,1)S(1)}, bf16[512,1024]{1,0:T(8,128)(2,1)}, u32[]{:S(2)}) copy-start(bf16[512,1024]{1,0:T(8,128)(2,1)} %pad_maximum_fusion.2) | copy-start | bytes 3145732
  176.4 5.2 %copy-start.39 = (bf16[512,512]{1,0:T(8,128)(2,1)S(1)}, bf16[512,512]{1,0:T(8,128)(2,1)}, u32[]{:S(2)}) copy-start(bf16[512,512]{1,0:T(8,128)(2,1)} %get-tuple-element.135) | copy-start | bytes 1572868
  176.4 13.5 %collective-permute-start.17 = (bf16[256,1024]{1,0:T(8,128)(2,1)}, bf16[256,1024]{1,0:T(8,128)(2,1)}, u32[]{:S(2)}, u32[]{:S(2)}) collective-permute-start(bf16[256,1024]{1,0:T(8,128)(2,1)} %fusion.12), channel_id=1, source_target_pairs={{0,2},{1,3},{2,0},{3,1},{4,6},{5,7},{6,4},{7,5},{8,10},{9,11},{10,... | collective-permute-start | bytes 1572872 | tf_op jit(solution)/shard_map/ppermute | solution.py:23
  177.9 13.2 %collective-permute-start.18 = (bf16[256,1024]{1,0:T(8,128)(2,1)}, bf16[256,1024]{1,0:T(8,128)(2,1)}, u32[]{:S(2)}, u32[]{:S(2)}) collective-permute-start(bf16[256,1024]{1,0:T(8,128)(2,1)} %add_convert_fusion.10), channel_id=1, source_target_pairs={{0,4},{4,0},{1,5},{5,1},{2,6},{6,2},{3,7},{7,3},{8,12},{12,8},{9,1... | collective-permute-start | bytes 1572872 | tf_op jit(solution)/shard_map/ppermute | solution.py:23
  193.3 2.3 collective-permute-start.19
  194.8 86.3 %reduce-scatter.9.cloned.1.call-start = ((), (), s32[]{:S(2)}) async-start(), calls=%async_computation.10 | async-start | bytes 983040 | tf_op jit(solution)/shard_map/reduce_scatter | solution.py:97
  211.1 5.6 %collective-permute-start.20 = (bf16[512,128]{1,0:T(8,128)(2,1)S(1)}, bf16[512,128]{1,0:T(8,128)(2,1)S(1)}, u32[]{:S(2)}, u32[]{:S(2)}) collective-permute-start(bf16[512,128]{1,0:T(8,128)(2,1)S(1)} %constant_dynamic-slice_fusion), channel_id=1, source_target_pairs={{0,4},{4,0},{1,5},{5,1},{2,6},{6,2},{3,7},{7,3},{8,12},{12,8},{9,1... | collective-permute-start | bytes 393224 | tf_op jit(solution)/shard_map/ppermute | solution.py:23
  215.2 21.1 %collective-permute-start.25 = (bf16[256,1024]{1,0:T(8,128)(2,1)}, bf16[256,1024]{1,0:T(8,128)(2,1)}, u32[]{:S(2)}, u32[]{:S(2)}) collective-permute-start(bf16[256,1024]{1,0:T(8,128)(2,1)} %add_convert_fusion.6), channel_id=1, source_target_pairs={{0,2},{1,3},{2,0},{3,1},{4,6},{5,7},{6,4},{7,5},{8,10},{9,11},{10,... | collective-permute-start | bytes 1572872 | tf_op jit(solution)/shard_map/ppermute | solution.py:23
  225.0 3.3 %collective-permute-start.21 = (bf16[256,1024]{1,0:T(8,128)(2,1)}, bf16[256,1024]{1,0:T(8,128)(2,1)}, u32[]{:S(2)}, u32[]{:S(2)}) collective-permute-start(bf16[256,1024]{1,0:T(8,128)(2,1)} %convolution_convert_fusion.2), channel_id=1, source_target_pairs={{0,1},{1,0},{2,3},{3,2},{4,5},{5,4},{6,7},{7,6},{8,9},{9,8},{10,11... | collective-permute-start | bytes 1572872 | tf_op jit(solution)/shard_map/ppermute | solution.py:23
  226.3 8.7 %collective-permute-start.23 = (bf16[256,1024]{1,0:T(8,128)(2,1)}, bf16[256,1024]{1,0:T(8,128)(2,1)S(1)}, u32[]{:S(2)}, u32[]{:S(2)}) collective-permute-start(bf16[256,1024]{1,0:T(8,128)(2,1)} %convolution_convert_fusion.1), channel_id=1, source_target_pairs={{0,1},{1,0},{2,3},{3,2},{4,5},{5,4},{6,7},{7,6},{8,9},{9,8},{10,11... | collective-permute-start | bytes 1572872 | tf_op jit(solution)/shard_map/ppermute | solution.py:23
  226.8 9.5 %collective-permute-start.24 = (bf16[512,256]{1,0:T(8,128)(2,1)}, bf16[512,256]{1,0:T(8,128)(2,1)}, u32[]{:S(2)}, u32[]{:S(2)}) collective-permute-start(bf16[512,256]{1,0:T(8,128)(2,1)} %bitcast.37), channel_id=1, source_target_pairs={{0,4},{4,0},{1,5},{5,1},{2,6},{6,2},{3,7},{7,3},{8,12},{12,8},{9,1... | collective-permute-start | bytes 786440 | tf_op jit(solution)/shard_map/ppermute | solution.py:23
  230.7 15.9 %collective-permute-start.22 = (bf16[256,1024]{1,0:T(8,128)(2,1)}, bf16[256,1024]{1,0:T(8,128)(2,1)}, u32[]{:S(2)}, u32[]{:S(2)}) collective-permute-start(bf16[256,1024]{1,0:T(8,128)(2,1)} %add_convert_fusion.8), channel_id=1, source_target_pairs={{0,4},{4,0},{1,5},{5,1},{2,6},{6,2},{3,7},{7,3},{8,12},{12,8},{9,1... | collective-permute-start | bytes 1572872 | tf_op jit(solution)/shard_map/ppermute | solution.py:23
  235.5 14.6 %copy-start.20 = (f32[512,1024]{1,0:T(8,128)S(1)}, f32[512,1024]{1,0:T(8,128)}, u32[]{:S(2)}) copy-start(f32[512,1024]{1,0:T(8,128)} %get-tuple-element.257) | copy-start | bytes 6291460
  248.7 17.4 %collective-permute-start.26 = (bf16[256,1024]{1,0:T(8,128)(2,1)}, bf16[256,1024]{1,0:T(8,128)(2,1)}, u32[]{:S(2)}, u32[]{:S(2)}) collective-permute-start(bf16[256,1024]{1,0:T(8,128)(2,1)} %add_convert_fusion.5), channel_id=1, source_target_pairs={{0,2},{1,3},{2,0},{3,1},{4,6},{5,7},{6,4},{7,5},{8,10},{9,11},{10,... | collective-permute-start | bytes 1572872 | tf_op jit(solution)/shard_map/ppermute | solution.py:23
  252.4 13.7 %all-to-all-start.1 = ((f32[8,32,128]{2,1,0:T(8,128)}), f32[8,32,128]{2,1,0:T(8,128)S(1)}, u32[]{:S(2)}, u32[]{:S(2)}) async-start(f32[8,32,128]{2,1,0:T(8,128)} %copy.96), calls=%async_computation.3 | async-start | bytes 262144 | tf_op jit(solution)/shard_map/all_to_all | solution.py:532
  255.9 38.7 %reduce-scatter.11.cloned.1.call-start = ((), (), s32[]{:S(2)}) async-start(), calls=%async_computation.11 | async-start | bytes 327680 | tf_op jit(solution)/shard_map/reduce_scatter | solution.py:97
  256.2 11.0 %copy-start.28 = (bf16[256,1024]{1,0:T(8,128)(2,1)S(1)}, bf16[256,1024]{1,0:T(8,128)(2,1)}, u32[]{:S(2)}) copy-start(bf16[256,1024]{1,0:T(8,128)(2,1)} %add_convert_fusion.5) | copy-start | bytes 1572868
  257.5 8.6 %collective-permute-start.30 = (bf16[2,128,512]{2,1,0:T(8,128)(2,1)S(1)}, bf16[2,128,512]{2,1,0:T(8,128)(2,1)}, u32[]{:S(2)}, u32[]{:S(2)}) collective-permute-start(bf16[2,128,512]{2,1,0:T(8,128)(2,1)S(1)} %get-tuple-element.274), channel_id=1, source_target_pairs={{0,4},{4,0},{1,5},{5,1},{2,6},{6,2},{3,7},{7,3},{8,12},{12,8},{9,1... | collective-permute-start | bytes 786440 | tf_op jit(solution)/shard_map/ppermute | solution.py:23
  266.1 3.4 %collective-permute-start.31 = (f32[2,128]{1,0:T(2,128)S(1)}, f32[2,128]{1,0:T(2,128)S(1)}, u32[]{:S(2)}, u32[]{:S(2)}) collective-permute-start(f32[2,128]{1,0:T(2,128)S(1)} %slice.132), channel_id=1, source_target_pairs={{0,1},{1,0},{2,3},{3,2},{4,5},{5,4},{6,7},{7,6},{8,9},{9,8},{10,11... | collective-permute-start | bytes 3080 | tf_op jit(solution)/shard_map/ppermute | solution.py:23
  269.0 5.7 %collective-permute-start.28 = (bf16[256,1024]{1,0:T(8,128)(2,1)S(1)}, bf16[256,1024]{1,0:T(8,128)(2,1)}, u32[]{:S(2)}, u32[]{:S(2)}) collective-permute-start(bf16[256,1024]{1,0:T(8,128)(2,1)S(1)} %fusion.26), channel_id=1, source_target_pairs={{0,1},{1,0},{2,3},{3,2},{4,5},{5,4},{6,7},{7,6},{8,9},{9,8},{10,11... | collective-permute-start | bytes 1572872 | tf_op jit(solution)/shard_map/ppermute | solution.py:23
  269.4 4.7 %collective-permute-start.32 = (f32[2,128]{1,0:T(2,128)S(1)}, f32[2,128]{1,0:T(2,128)S(1)}, u32[]{:S(2)}, u32[]{:S(2)}) collective-permute-start(f32[2,128]{1,0:T(2,128)S(1)} %slice_add_fusion), channel_id=1, source_target_pairs={{0,2},{1,3},{2,0},{3,1},{4,6},{5,7},{6,4},{7,5},{8,10},{9,11},{10,... | collective-permute-start | bytes 3080 | tf_op jit(solution)/shard_map/ppermute | solution.py:23
  272.4 4.2 %collective-permute-start.27 = (bf16[256,1024]{1,0:T(8,128)(2,1)S(1)}, bf16[256,1024]{1,0:T(8,128)(2,1)}, u32[]{:S(2)}, u32[]{:S(2)}) collective-permute-start(bf16[256,1024]{1,0:T(8,128)(2,1)S(1)} %add_convert_fusion.4), channel_id=1, source_target_pairs={{0,1},{1,0},{2,3},{3,2},{4,5},{5,4},{6,7},{7,6},{8,9},{9,8},{10,11... | collective-permute-start | bytes 1572872 | tf_op jit(solution)/shard_map/ppermute | solution.py:23
  282.1 14.1 %collective-permute-start.29 = (bf16[128,384]{1,0:T(8,128)(2,1)S(1)}, bf16[128,384]{1,0:T(8,128)(2,1)S(1)}, u32[]{:S(2)}, u32[]{:S(2)}) collective-permute-start(bf16[128,384]{1,0:T(8,128)(2,1)S(1)} %dynamic-slice_convert_fusion), channel_id=1, source_target_pairs={{0,4},{4,0},{1,5},{5,1},{2,6},{6,2},{3,7},{7,3},{8,12},{12,8},{9,1... | collective-permute-start | bytes 294920 | tf_op jit(solution)/shard_map/ppermute | solution.py:23
  (22 other events, 44.7 us)
Sparse Core Ops, SparseCore 0:
  60.0 26.1 all-gather.2
  105.1 27.5 all-gather.4
  173.4 26.9 reduce-scatter.4
  203.2 25.7 reduce-scatter.6
  248.7 24.0 reduce-scatter.8
  275.5 19.0 reduce-scatter.10
where the time goes:
time: 309 us; the launch traced here: 305 us
  waiting for transfers between devices  118 us (38%)
  other arithmetic  56.4 us (18%)
  matrix products  42.5 us (14%)
  starting transfers between devices  36.9 us (12%)
  local copies, waits for them, and re-layouts  21.1 us (7%)
  between operations  15.3 us (5%)
  Pallas kernels  14.8 us (5%)
    ppermute x33, waiting for transfers between devices, swap(): return lax.ppermute(array, axis, [(i, i ^ mask) for i in range(devices)])  70.2 us
    dot_general x25, matrix products, dot(): lax.dot_general(left, right, (((left_dim,), (right_dim,)), ((), ())), pre...  42.5 us
    ppermute x33, starting transfers between devices, swap(): return lax.ppermute(array, axis, [(i, i ^ mask) for i in range(devices)])  27.8 us
    all_gather x2, waiting for transfers between devices, gather_rows(): return lax.all_gather(block, 'fsdp', axis=0, tiled=True)  27.4 us
    reduce_scatter x4, waiting for transfers between devices, scatter_rows(): return lax.psum_scatter(array, 'fsdp', scatter_dimension=0, tiled=True)  11.3 us
    reduce_sum x1, other arithmetic, local(): grad_out_bias = jnp.sum(grad_branch_low.astype(jnp.float32), axis=0)  11 us
    convert_element_type x6, other arithmetic, pair_sum(): (kept.astype(jnp.float32) + sent.astype(jnp.float32)).astype(jnp.bfloat16)  10.7 us
    unnamed x97, local copies, waits for them, and re-layouts  10.1 us
  transfers between devices with their start and end apart: 41, of which 21 were waited for; matrix products, arithmetic and copies ran while one was open for 33% of the time, Pallas kernels for 5%

commit v1 on v0

--- a/solution.py
+++ b/solution.py
@@ -294,7 +294,6 @@
 
     both_packs = jnp.stack(ordered(ctx_place, own_pack, other_pack))
     packs = gather_fsdp(both_packs)
-    packs, ffn_pair = lax.optimization_barrier((packs, ffn_pair))
     up_full = gather_rows(ffn_pair[:, :drow].reshape(-1, part_hidden))
     down_full = gather_rows(ffn_pair[:, drow:].reshape(-1, part_hidden))
     packs = packs.reshape(owners, -1, LANES)
@@ -335,9 +334,7 @@
         return ordered(ctx_place, kept, sent)
 
     attended = to_tokens(attended_part)
-    attended, up_full, grad_got, grad_turned = lax.optimization_barrier(
-        (attended, up_full, grad_got, grad_turned)
-    )
+    attended, grad_got, grad_turned = lax.optimization_barrier((attended, grad_got, grad_turned))
     attended = jnp.concatenate(attended, axis=1)
     inputs = own_tokens.astype(jnp.float32)
 
@@ -345,16 +342,16 @@
         return dot(lax.dynamic_slice_in_dim(attended, start, count, 0), out_full, 1, 1)
 
     def small_vectors(gated, unused):
-        smalls = gated
+        smalls, up_full = gated
         vectors = smalls[:, :8, :drow].transpose(1, 0, 2).reshape(8, width)
         up_bias = lax.dynamic_slice_in_dim(
             smalls[:, 16 : 16 + up_rows, :hrow], ctx_place * (up_rows // 2), up_rows // 2, 1
         )
         up_bias = up_bias.transpose(1, 0, 2).reshape(1, -1)
-        return (vectors, up_bias), ()
-
-    attn_sum, (vectors, up_bias_part), unused = sum_tp(
-        out_part, block_len, core_place, small_vectors, smalls
+        return (vectors, up_bias, up_full), ()
+
+    attn_sum, (vectors, up_bias_part, up_full), unused = sum_tp(
+        out_part, block_len, core_place, small_vectors, (smalls, up_full)
     )
     gain_one, shift_one, gain_two, shift_two, out_bias, down_bias = (vectors[i] for i in range(6))
     middle = inputs + (attn_sum.astype(jnp.float32) + out_bias)
@@ -368,18 +365,16 @@
         return gelu_pull(grad_activated)[0].astype(jnp.bfloat16)
 
     half_rows = lax.dynamic_slice_in_dim(normed_two, core_place * half, half, 0)
-    half_rows, late_normed, down_full = lax.optimization_barrier(
-        (half_rows, normed_two, down_full)
-    )
+    half_rows, late_normed = lax.optimization_barrier((half_rows, normed_two))
     got = swap(half_rows, "ctx")
     own_pre = hidden(late_normed)
     own_active = gelu_tanh(own_pre).astype(jnp.bfloat16)
+    other_grad = jnp.concatenate([grad_got, grad_turned])
+    got, own_pre, own_active, other_grad, down_full = lax.optimization_barrier(
+        (got, own_pre, own_active, other_grad, down_full)
+    )
+    other_normed = jnp.concatenate([got, swap(got, "tp", CORE)])
     own_hidden = hidden_grad(own_pre, own_grad)
-    other_grad = jnp.concatenate([grad_got, grad_turned])
-    got, own_hidden, own_active, other_grad = lax.optimization_barrier(
-        (got, own_hidden, own_active, other_grad)
-    )
-    other_normed = jnp.concatenate([got, swap(got, "tp", CORE)])
     other_pre = hidden(other_normed)
     other_active = gelu_tanh(other_pre).astype(jnp.bfloat16)
     other_hidden = hidden_grad(other_pre, other_grad)
@@ -467,13 +462,13 @@
     first_kept = chip_sum_rows(
         token_rows(ctx_place, 1 - core_place), token_rows(ctx_place, core_place), qkv_part
     )
-    first_sent, late_part = lax.optimization_barrier((first_sent, grad_qkv_part))
+    first_sent, late_part, got_out = lax.optimization_barrier(
+        (first_sent, grad_qkv_part, got_out)
+    )
     first_got = swap(first_sent, "ctx")
     grad_qkv_weight = dot(normed_all, late_part, 0, 0).astype(jnp.bfloat16)
-    first_got, first_kept, grad_qkv_weight, kept_out, got_out, mlp_across, mlp_pair = (
-        lax.optimization_barrier(
-            (first_got, first_kept, grad_qkv_weight, kept_out, got_out, mlp_across, mlp_pair)
-        )
+    first_got, first_kept, kept_out, got_out, mlp_across, mlp_pair = lax.optimization_barrier(
+        (first_got, first_kept, kept_out, got_out, mlp_across, mlp_pair)
     )
     grad_qkv_sum = row_major(scatter_rows(grad_qkv_weight)).astype(jnp.float32)
     own_rows = lax.dynamic_slice_in_dim(grad_qkv_sum, ctx_place * drow, drow, 0)

time: 309 us -> 319 us (1.032)
  waiting for transfers between devices: 118 us -> 129 us
  matrix products: 42.5 us -> 37 us
    all_gather x2, waiting for transfers between devices: 27.4 us -> 35.4 us  [gather_rows(): return lax.all_gather(block, 'fsdp', axis=0, tiled=True)]
    dot_general x25, matrix products: 42.5 us -> 37 us  [dot(): lax.dot_general(left, right, (((left_dim,), (right_dim,)), ((), ())), pre...]
    ppermute x33, waiting for transfers between devices: 70.2 us -> 75.4 us  [swap(): return lax.ppermute(array, axis, [(i, i ^ mask) for i in range(devices)])]
    unnamed x97 -> x95, local copies, waits for them, and re-layouts: 10.1 us -> 12.2 us
  transfers between devices with their start and end apart: 41 -> 41, of which waited for: 21 -> 21; matrix products, arithmetic and copies ran while one was open for 33% -> 31% of each run, Pallas kernels for 5% -> 5%
where the time goes in v1:
time: 319 us; the launch traced here: 314 us
  waiting for transfers between devices  129 us (40%)
  other arithmetic  57.8 us (18%)
  starting transfers between devices  38.4 us (12%)
  matrix products  37 us (12%)
  local copies, waits for them, and re-layouts  21.7 us (7%)
  between operations  15.4 us (5%)
  Pallas kernels  14.8 us (5%)
    ppermute x33, waiting for transfers between devices, swap(): return lax.ppermute(array, axis, [(i, i ^ mask) for i in range(devices)])  75.4 us
    dot_general x25, matrix products, dot(): lax.dot_general(left, right, (((left_dim,), (right_dim,)), ((), ())), pre...  37 us
    all_gather x2, waiting for transfers between devices, gather_rows(): return lax.all_gather(block, 'fsdp', axis=0, tiled=True)  35.4 us
    ppermute x33, starting transfers between devices, swap(): return lax.ppermute(array, axis, [(i, i ^ mask) for i in range(devices)])  29.4 us
    unnamed x95, local copies, waits for them, and re-layouts  12.2 us
    reduce_sum x1, other arithmetic, local(): grad_out_bias = jnp.sum(grad_branch_low.astype(jnp.float32), axis=0)  11 us
    reduce_scatter x4, waiting for transfers between devices, scatter_rows(): return lax.psum_scatter(array, 'fsdp', scatter_dimension=0, tiled=True)  10.4 us
    convert_element_type x6, other arithmetic, pair_sum(): (kept.astype(jnp.float32) + sent.astype(jnp.float32)).astype(jnp.bfloat16)  9.65 us
  transfers between devices with their start and end apart: 41, of which 21 were waited for; matrix products, arithmetic and copies ran while one was open for 31% of the time, Pallas kernels for 5%

profile of v1, /device:TPU:0, one launch (start us, length us, event | category | flops | bytes accessed | tf_op | source)
XLA Modules:
  0.0 314.3 jit_solution(3982673214765452458)
XLA Ops:
  10.8 3.0 collective-permute-start
  13.8 4.4 %collective-permute-done = bf16[672,128]{1,0:T(8,128)(2,1)S(1)} collective-permute-done((bf16[672,128]{1,0:T(8,128)(2,1)S(1)}, bf16[672,128]{1,0:T(8,128)(2,1)S(1)}, u32[]{:S(2)}, u32[]{:S(2)}) %collective-permute-start) | collective-permute-done | bytes 172064 | tf_op jit(solution)/shard_map/ppermute | solution.py:23
  19.2 1.8 collective-permute-start.1
  21.1 11.3 %collective-permute-done.1 = bf16[256,1024]{1,0:T(8,128)(2,1)S(1)} collective-permute-done((bf16[256,1024]{1,0:T(8,128)(2,1)S(1)}, bf16[256,1024]{1,0:T(8,128)(2,1)S(1)}, u32[]{:S(2)}, u32[]{:S(2)}) %collective-permute-start.1) | collective-permute-done | bytes 524320 | tf_op jit(solution)/shard_map/ppermute | solution.py:23
  32.4 1.3 broadcast_in_dim.14
  33.7 4.9 %all-to-all-start = ((bf16[4,2,672,128]{3,2,1,0:T(8,128)(2,1)}), bf16[4,2,672,128]{3,2,1,0:T(8,128)(2,1)}, u32[]{:S(2)}, u32[]{:S(2)}) async-start(bf16[4,2,672,128]{3,2,1,0:T(8,128)(2,1)} %broadcast_in_dim.14), calls=%async_computation | async-start | bytes 2752512 | tf_op jit(solution)/shard_map/all_to_all | solution.py:32
  38.9 1.9 broadcast_select_fusion.1
  42.9 1.5 collective-permute-start.4
  45.3 17.5 %collective-permute-done.7 = bf16[256,512]{1,0:T(8,128)(2,1)S(1)} collective-permute-done((bf16[256,512]{1,0:T(8,128)(2,1)S(1)}, bf16[256,512]{1,0:T(8,128)(2,1)S(1)}, u32[]{:S(2)}, u32[]{:S(2)}) %collective-permute-start.7) | collective-permute-done | bytes 262176 | tf_op jit(solution)/shard_map/ppermute | solution.py:23
  62.8 2.0 select_bitcast_fusion.2
  64.8 7.4 %all-to-all-done = bf16[4,2,672,128]{3,2,1,0:T(8,128)(2,1)} async-done(((bf16[4,2,672,128]{3,2,1,0:T(8,128)(2,1)}), bf16[4,2,672,128]{3,2,1,0:T(8,128)(2,1)}, u32[]{:S(2)}, u32[]{:S(2)}) %all-to-all-start) | async-done | bytes 1376288 | tf_op jit(solution)/shard_map/all_to_all | solution.py:32
  73.7 7.8 %shard_map.254 = (bf16[1024,1024]{1,0:T(8,128)(2,1)S(1)}, bf16[1024,384]{1,0:T(8,128)(2,1)S(1)}, bf16[1024,128]{1,0:T(8,128)(2,1)S(1)}, bf16[1024,384]{1,0:T(8,128)(2,1)S(1)}, bf16[1024,256]{1,0:T(8,128)(2,1)S(1)}) custom-call(bf16[1024,1024]{1,0:T(8,128)(2,1)S(1)} %pad_maximum_fusion.tokens_ref, bf16[8,672,128]{2,1,0:T(8,128)(2,1)} %bitcast.16.packs_ref, ...), custom_call_target="tpu_custom_call" | custom-call | flops 805306368 | bytes 8388608 | tf_op jit(solution)/shard_map/pallas_call | solution.py:313
  82.3 1.3 copy-done.4
  85.2 1.6 collective-permute-start.3
  87.7 2.6 collective-permute-done.3
  91.7 1.9 collective-permute-done.6
  94.0 19.9 %all-gather.3.cloned.1.call-done = bf16[1024,512]{1,0:T(8,128)(2,1)} async-done(((bf16[256,512]{1,0:T(8,128)(2,1)}), bf16[1024,512]{1,0:T(8,128)(2,1)}) %all-gather.3.cloned.1.call-update) | async-done | bytes 1048592 | tf_op jit(solution)/shard_map/all_gather | solution.py:38
  113.9 1.5 collective-permute-start.8
  115.5 11.9 %collective-permute-done.8 = bf16[256,1024]{1,0:T(8,128)(2,1)S(1)} collective-permute-done((bf16[256,1024]{1,0:T(8,128)(2,1)S(1)}, bf16[256,1024]{1,0:T(8,128)(2,1)S(1)}, u32[]{:S(2)}, u32[]{:S(2)}) %collective-permute-start.8) | collective-permute-done | bytes 524320 | tf_op jit(solution)/shard_map/ppermute | solution.py:23
  128.8 1.4 dynamic-slice_reduce_fusion
  135.2 1.5 collective-permute-start.10
  136.6 2.2 pad_maximum_fusion.2
  138.9 2.1 fusion.31
  141.0 15.5 %all-gather.5.cloned.1.call-done = bf16[1024,512]{1,0:T(8,128)(2,1)} async-done(((bf16[256,512]{1,0:T(8,128)(2,1)}), bf16[1024,512]{1,0:T(8,128)(2,1)}) %all-gather.5.cloned.1.call-update) | async-done | bytes 1048592 | tf_op jit(solution)/shard_map/all_gather | solution.py:38
  157.8 2.2 fusion.81
  161.3 1.5 multiply_convert_fusion
  168.3 1.5 collective-permute-start.14
  169.7 1.3 convolution_convert_fusion.5
  171.0 1.3 convolution_convert_fusion.4
  173.6 1.8 add_convert_fusion.2
  175.3 2.8 fusion.10
  178.1 2.4 fusion.11
  180.5 1.9 collective-permute-done.14
  182.5 3.0 fusion.14
  185.5 1.5 collective-permute-start.17
  187.0 1.5 collective-permute-start.18
  189.6 1.9 fusion.84
  191.8 1.7 add_convert_fusion.1
  193.6 5.2 %collective-permute-done.17 = bf16[256,1024]{1,0:T(8,128)(2,1)} collective-permute-done((bf16[256,1024]{1,0:T(8,128)(2,1)}, bf16[256,1024]{1,0:T(8,128)(2,1)}, u32[]{:S(2)}, u32[]{:S(2)}) %collective-permute-start.17) | collective-permute-done | bytes 524320 | tf_op jit(solution)/shard_map/ppermute | solution.py:23
  200.0 2.2 add_convert_fusion.9
  202.2 1.5 multiply_reduce_fusion.3
  204.5 1.3 broadcast_select_fusion.7
  205.8 2.6 fusion.6
  208.4 11.0 %convert_reduce_fusion.2 = (f32[1024]{0:T(1024)S(1)}, bf16[512,1024]{1,0:T(8,128)(2,1)S(1)}, f32[512,1024]{1,0:T(8,128)}) fusion(f32[512]{0:T(512)S(1)} %broadcast_multiply_fusion.3, f32[512]{0:T(512)S(1)} %get-tuple-element.308, f32[1024]{0:T(1024)S(1)} %bitcast.185, bf16[256,1024]{1,0:T(8,128)(2,1)S(1)} %copy-done.13, bf16[256,1024]{1,0:T(8,128)(2,1)S(1)} %copy-done.10, ...), kind=kLoop, calls=%fused_computation.19 | loop fusion | flops 12057600 | bytes 7360512 | tf_op jit(solution)/shard_map/reduce_sum | solution.py:424
  219.9 1.5 collective-permute-start.20
  222.0 2.1 add_convert_fusion.6
  225.6 7.0 %shard_map.255 = (bf16[1024,384]{1,0:T(8,128)(2,1)S(1)}, f32[2,128]{1,0:T(2,128)S(1)}) custom-call(bf16[1024,384]{1,0:T(8,128)(2,1)S(1)} %copy-done.6, bf16[1024,128]{1,0:T(8,128)(2,1)S(1)} %pad_maximum_fusion.10.grad_ref, s32[1,1024]{1,0:T(1,128)S(1)} %copy-done.3, s32[1024,1]{1,0:T(8,128)S(1)} %copy.90.seg_col_ref), custom_call_target="tpu_custom_call" | custom-call | flops 1342177280 | bytes 2097152 | tf_op jit(solution)/shard_map/pallas_call | solution.py:440
  233.9 1.5 collective-permute-start.22
  238.3 4.7 %collective-permute-done.22 = bf16[512,256]{1,0:T(8,128)(2,1)} collective-permute-done((bf16[512,256]{1,0:T(8,128)(2,1)}, bf16[512,256]{1,0:T(8,128)(2,1)}, u32[]{:S(2)}, u32[]{:S(2)}) %collective-permute-start.22) | collective-permute-done | bytes 262176 | tf_op jit(solution)/shard_map/ppermute | solution.py:23
  243.0 1.5 collective-permute-start.23
  244.4 3.8 %convolution_convert_fusion = bf16[1024,384]{1,0:T(8,128)(2,1)} fusion(bf16[1024,1024]{1,0:T(8,128)(2,1)} %copy-done.4, bf16[1024,384]{1,0:T(8,128)(2,1)S(1)} %get-tuple-element.172), kind=kOutput, calls=%fused_computation.39 | convolution fusion | flops 805699584 | bytes 3670016 | tf_op jit(solution)/shard_map/dot_general | solution.py:126
  248.2 1.5 add_convert_fusion.7
  249.8 7.1 %collective-permute-done.23 = bf16[256,1024]{1,0:T(8,128)(2,1)} collective-permute-done((bf16[256,1024]{1,0:T(8,128)(2,1)}, bf16[256,1024]{1,0:T(8,128)(2,1)}, u32[]{:S(2)}, u32[]{:S(2)}) %collective-permute-start.23) | collective-permute-done | bytes 524320 | tf_op jit(solution)/shard_map/ppermute | solution.py:23
  258.1 1.4 collective-permute-start.26
  259.6 1.5 fusion.34
  262.0 3.4 %all-to-all-start.1 = ((f32[8,32,128]{2,1,0:T(8,128)}), f32[8,32,128]{2,1,0:T(8,128)S(1)}, u32[]{:S(2)}, u32[]{:S(2)}) async-start(f32[8,32,128]{2,1,0:T(8,128)} %copy.96), calls=%async_computation.3 | async-start | bytes 262144 | tf_op jit(solution)/shard_map/all_to_all | solution.py:527
  266.4 1.9 collective-permute-start.30
  268.3 2.2 add_convert_fusion.4
  270.5 1.7 add_convert_fusion.12
  281.7 1.6 collective-permute-start.29
  283.8 3.2 %collective-permute-done.29 = bf16[128,384]{1,0:T(8,128)(2,1)S(1)} collective-permute-done((bf16[128,384]{1,0:T(8,128)(2,1)S(1)}, bf16[128,384]{1,0:T(8,128)(2,1)S(1)}, u32[]{:S(2)}, u32[]{:S(2)}) %collective-permute-start.29) | collective-permute-done | bytes 98336 | tf_op jit(solution)/shard_map/ppermute | solution.py:23
  290.2 10.3 %reduce-scatter.11.cloned.1.call-done = bf16[128,256]{1,0:T(8,128)(2,1)} async-done(((bf16[512,256]{1,0:T(8,128)(2,1)}), bf16[128,256]{1,0:T(8,128)(2,1)}) %reduce-scatter.11.cloned.1.call-update) | async-done | bytes 65552 | tf_op jit(solution)/shard_map/reduce_scatter | solution.py:97
  302.1 1.4 broadcast_select_fusion.5
  304.0 3.3 %add_bitcast_fusion = (f32[1,512,1024]{2,1,0:T(8,128)}, bf16[1,512,1024]{2,1,0:T(8,128)(2,1)}) fusion(f32[512,1024]{1,0:T(8,128)S(1)} %copy-done.23, bf16[512,1024]{1,0:T(8,128)(2,1)S(1)} %bitcast.163, f32[512]{0:T(512)S(1)} %broadcast_multiply_fusion, f32[512]{0:T(512)S(1)} %broadcast_multiply_fusion.1, f32[1024]{0:T(1024)S(1)} %bitcast.193, ...), kind=kLoop, calls=%fused_computation.13 | loop fusion | flops 13631488 | bytes 9457664 | tf_op jit(solution)/shard_map/broadcast_in_dim | solution.py:565
  (253 shorter events, 58.4 us)
Async XLA Ops:
  10.8 7.4 %collective-permute-start = (bf16[672,128]{1,0:T(8,128)(2,1)S(1)}, bf16[672,128]{1,0:T(8,128)(2,1)S(1)}, u32[]{:S(2)}, u32[]{:S(2)}) collective-permute-start(bf16[672,128]{1,0:T(8,128)(2,1)S(1)} %pad_maximum_fusion.14), channel_id=1, source_target_pairs={{0,4},{4,0},{1,5},{5,1},{2,6},{6,2},{3,7},{7,3},{8,12},{12,8},{9,1... | collective-permute-start | bytes 516104 | tf_op jit(solution)/shard_map/ppermute | solution.py:23
  19.2 13.2 %collective-permute-start.1 = (bf16[256,1024]{1,0:T(8,128)(2,1)S(1)}, bf16[256,1024]{1,0:T(8,128)(2,1)S(1)}, u32[]{:S(2)}, u32[]{:S(2)}) collective-permute-start(bf16[256,1024]{1,0:T(8,128)(2,1)S(1)} %constant_dynamic-slice_fusion.6), channel_id=1, source_target_pairs={{0,4},{4,0},{1,5},{5,1},{2,6},{6,2},{3,7},{7,3},{8,12},{12,8},{9,1... | collective-permute-start | bytes 1572872 | tf_op jit(solution)/shard_map/ppermute | solution.py:23
  32.4 6.4 %collective-permute-start.2 = (bf16[256,1024]{1,0:T(8,128)(2,1)S(1)}, bf16[256,1024]{1,0:T(8,128)(2,1)S(1)}, u32[]{:S(2)}, u32[]{:S(2)}) collective-permute-start(bf16[256,1024]{1,0:T(8,128)(2,1)S(1)} %collective-permute-done.1), channel_id=1, source_target_pairs={{0,1},{1,0},{2,3},{3,2},{4,5},{5,4},{6,7},{7,6},{8,9},{9,8},{10,11... | collective-permute-start | bytes 1572872 | tf_op jit(solution)/shard_map/ppermute | solution.py:23
  32.4 6.2 %copy-start.41 = (bf16[1024,128]{1,0:T(8,128)(2,1)S(1)}, bf16[1024,128]{1,0:T(8,128)(2,1)}, u32[]{:S(2)}) copy-start(bf16[1024,128]{1,0:T(8,128)(2,1)} %param.23) | copy-start | bytes 786436
  33.7 5.2 %copy-start.7 = (bf16[1,512,1024]{2,1,0:T(8,128)(2,1)S(1)}, bf16[1,512,1024]{2,1,0:T(8,128)(2,1)}, u32[]{:S(2)}) copy-start(bf16[1,512,1024]{2,1,0:T(8,128)(2,1)} %param.15) | copy-start | bytes 3145732
  33.7 38.5 %all-to-all-start = ((bf16[4,2,672,128]{3,2,1,0:T(8,128)(2,1)}), bf16[4,2,672,128]{3,2,1,0:T(8,128)(2,1)}, u32[]{:S(2)}, u32[]{:S(2)}) async-start(bf16[4,2,672,128]{3,2,1,0:T(8,128)(2,1)} %broadcast_in_dim.14), calls=%async_computation | async-start | bytes 2752512 | tf_op jit(solution)/shard_map/all_to_all | solution.py:32
  38.7 75.2 %all-gather.3.cloned.1.call-start = ((), (), s32[]{:S(2)}) async-start(), calls=%async_computation.6 | async-start | bytes 1310720 | tf_op jit(solution)/shard_map/all_gather | solution.py:38
  38.8 5.6 %copy-start.30 = (bf16[1024,128]{0,1:T(8,128)(2,1)}, bf16[1024,128]{0,1:T(8,128)(2,1)S(1)}, u32[]{:S(2)}) copy-start(bf16[1024,128]{0,1:T(8,128)(2,1)S(1)} %copy.91) | copy-start | bytes 786436
  40.9 4.2 %copy-start.3 = (s32[1,1024]{1,0:T(1,128)S(1)}, s32[1,1024]{1,0:T(1,128)}, u32[]{:S(2)}) copy-start(s32[1,1024]{1,0:T(1,128)} %seg_row_ref.3) | copy-start | bytes 12292
  42.9 21.9 %collective-permute-start.4 = (bf16[256,1024]{1,0:T(8,128)(2,1)}, bf16[256,1024]{1,0:T(8,128)(2,1)}, u32[]{:S(2)}, u32[]{:S(2)}) collective-permute-start(bf16[256,1024]{1,0:T(8,128)(2,1)} %constant_dynamic-slice_fusion.2), channel_id=1, source_target_pairs={{0,4},{4,0},{1,5},{5,1},{2,6},{6,2},{3,7},{7,3},{8,12},{12,8},{9,1... | collective-permute-start | bytes 1572872 | tf_op jit(solution)/shard_map/ppermute | solution.py:23
  44.4 18.4 %collective-permute-start.7 = (bf16[256,512]{1,0:T(8,128)(2,1)S(1)}, bf16[256,512]{1,0:T(8,128)(2,1)S(1)}, u32[]{:S(2)}, u32[]{:S(2)}) collective-permute-start(bf16[256,512]{1,0:T(8,128)(2,1)S(1)} %fusion.42), channel_id=1, source_target_pairs={{0,4},{4,0},{1,5},{5,1},{2,6},{6,2},{3,7},{7,3},{8,12},{12,8},{9,1... | collective-permute-start | bytes 786440 | tf_op jit(solution)/shard_map/ppermute | solution.py:23
  64.8 26.4 %collective-permute-start.5 = (bf16[256,1024]{1,0:T(8,128)(2,1)}, bf16[256,1024]{1,0:T(8,128)(2,1)}, u32[]{:S(2)}, u32[]{:S(2)}) collective-permute-start(bf16[256,1024]{1,0:T(8,128)(2,1)} %collective-permute-done.4), channel_id=1, source_target_pairs={{0,1},{1,0},{2,3},{3,2},{4,5},{5,4},{6,7},{7,6},{8,9},{9,8},{10,11... | collective-permute-start | bytes 1572872 | tf_op jit(solution)/shard_map/ppermute | solution.py:23
  73.7 13.1 %copy-start.37 = (bf16[1,256,512]{2,1,0:T(8,128)(2,1)S(1)}, bf16[1,256,512]{2,1,0:T(8,128)(2,1)}, u32[]{:S(2)}) copy-start(bf16[1,256,512]{2,1,0:T(8,128)(2,1)} %get-tuple-element.264) | copy-start | bytes 786436
  73.7 13.1 %copy-start.38 = (bf16[1,256,512]{2,1,0:T(8,128)(2,1)S(1)}, bf16[1,256,512]{2,1,0:T(8,128)(2,1)}, u32[]{:S(2)}) copy-start(bf16[1,256,512]{2,1,0:T(8,128)(2,1)} %get-tuple-element.265) | copy-start | bytes 786436
  85.2 6.1 %copy-start.1 = (bf16[1024,256]{1,0:T(8,128)(2,1)S(1)}, bf16[1024,256]{1,0:T(8,128)(2,1)}, u32[]{:S(2)}) copy-start(bf16[1024,256]{1,0:T(8,128)(2,1)} %copy-done) | copy-start | bytes 1572868
  85.2 5.0 %collective-permute-start.3 = (bf16[512,128]{1,0:T(8,128)(2,1)S(1)}, bf16[512,128]{1,0:T(8,128)(2,1)S(1)}, u32[]{:S(2)}, u32[]{:S(2)}) collective-permute-start(bf16[512,128]{1,0:T(8,128)(2,1)S(1)} %constant_dynamic-slice_fusion.3), channel_id=1, source_target_pairs={{0,4},{4,0},{1,5},{5,1},{2,6},{6,2},{3,7},{7,3},{8,12},{12,8},{9,1... | collective-permute-start | bytes 393224 | tf_op jit(solution)/shard_map/ppermute | solution.py:23
  87.6 27.8 %copy-start.40 = (f32[8,32,128]{2,1,0:T(8,128)S(1)}, f32[8,32,128]{2,1,0:T(8,128)}, u32[]{:S(2)}) copy-start(f32[8,32,128]{2,1,0:T(8,128)} %copy-done.39) | copy-start | bytes 393220
  87.6 68.8 %all-gather.5.cloned.1.call-start = ((), (), s32[]{:S(2)}) async-start(), calls=%async_computation.7 | async-start | bytes 1310720 | tf_op jit(solution)/shard_map/all_gather | solution.py:38
  91.7 2.0 collective-permute-start.6
  113.9 13.5 %collective-permute-start.8 = (bf16[256,1024]{1,0:T(8,128)(2,1)S(1)}, bf16[256,1024]{1,0:T(8,128)(2,1)S(1)}, u32[]{:S(2)}, u32[]{:S(2)}) collective-permute-start(bf16[256,1024]{1,0:T(8,128)(2,1)S(1)} %add_convert_fusion.11), channel_id=1, source_target_pairs={{0,2},{1,3},{2,0},{3,1},{4,6},{5,7},{6,4},{7,5},{8,10},{9,11},{10,... | collective-permute-start | bytes 1572872 | tf_op jit(solution)/shard_map/ppermute | solution.py:23
  128.4 2.3 collective-permute-start.9
  128.4 129.6 %reduce-scatter.5.cloned.1.call-start = ((), (), s32[]{:S(2)}) async-start(), calls=%async_computation.8 | async-start | bytes 1310720 | tf_op jit(solution)/shard_map/reduce_scatter | solution.py:97
  134.3 4.6 %copy-start.24 = (bf16[512,1024]{1,0:T(8,128)(2,1)}, bf16[512,1024]{1,0:T(8,128)(2,1)S(1)}, u32[]{:S(2)}) copy-start(bf16[512,1024]{1,0:T(8,128)(2,1)S(1)} %add_convert_fusion.3) | copy-start | bytes 3145732
  134.3 4.6 %copy-start.15 = (bf16[1024,512]{1,0:T(8,128)(2,1)S(1)}, bf16[1024,512]{1,0:T(8,128)(2,1)}, u32[]{:S(2)}) copy-start(bf16[1024,512]{1,0:T(8,128)(2,1)} %all-gather.3.cloned.1.call-done) | copy-start | bytes 3145732
  135.2 21.3 %collective-permute-start.10 = (bf16[256,1024]{1,0:T(8,128)(2,1)}, bf16[256,1024]{1,0:T(8,128)(2,1)}, u32[]{:S(2)}, u32[]{:S(2)}) collective-permute-start(bf16[256,1024]{1,0:T(8,128)(2,1)} %constant_dynamic-slice_fusion.1), channel_id=1, source_target_pairs={{0,4},{4,0},{1,5},{5,1},{2,6},{6,2},{3,7},{7,3},{8,12},{12,8},{9,1... | collective-permute-start | bytes 1572872 | tf_op jit(solution)/shard_map/ppermute | solution.py:23
  156.5 3.6 %copy-start.28 = (bf16[512,1024]{1,0:T(8,128)(2,1)S(1)}, bf16[512,1024]{1,0:T(8,128)(2,1)}, u32[]{:S(2)}) copy-start(bf16[512,1024]{1,0:T(8,128)(2,1)} %pad_maximum_fusion.2) | copy-start | bytes 3145732
  157.7 3.1 collective-permute-start.12
  162.8 8.2 %copy-start.32 = (bf16[512,512]{1,0:T(8,128)(2,1)}, bf16[512,512]{1,0:T(8,128)(2,1)S(1)}, u32[]{:S(2)}) copy-start(bf16[512,512]{1,0:T(8,128)(2,1)S(1)} %get-tuple-element.133) | copy-start | bytes 1572868
  162.8 10.8 %copy-start.26 = (bf16[512,512]{1,0:T(8,128)(2,1)}, bf16[512,512]{1,0:T(8,128)(2,1)S(1)}, u32[]{:S(2)}) copy-start(bf16[512,512]{1,0:T(8,128)(2,1)S(1)} %get-tuple-element.135) | copy-start | bytes 1572868
  163.3 3.7 %collective-permute-start.13 = (bf16[256,1024]{1,0:T(8,128)(2,1)S(1)}, bf16[256,1024]{1,0:T(8,128)(2,1)S(1)}, u32[]{:S(2)}, u32[]{:S(2)}) collective-permute-start(bf16[256,1024]{1,0:T(8,128)(2,1)S(1)} %convolution_convert_fusion.6), channel_id=1, source_target_pairs={{0,1},{1,0},{2,3},{3,2},{4,5},{5,4},{6,7},{7,6},{8,9},{9,8},{10,11... | collective-permute-start | bytes 1572872 | tf_op jit(solution)/shard_map/ppermute | solution.py:23
  165.2 7.6 %copy-start.22 = (bf16[512,512]{1,0:T(8,128)(2,1)}, bf16[512,512]{1,0:T(8,128)(2,1)S(1)}, u32[]{:S(2)}) copy-start(bf16[512,512]{1,0:T(8,128)(2,1)S(1)} %fusion.32) | copy-start | bytes 1572868
  165.2 4.5 %copy-start.34 = (bf16[512,512]{1,0:T(8,128)(2,1)S(1)}, bf16[512,512]{1,0:T(8,128)(2,1)}, u32[]{:S(2)}) copy-start(bf16[512,512]{1,0:T(8,128)(2,1)} %get-tuple-element.132) | copy-start | bytes 1572868
  166.5 16.0 %collective-permute-start.11 = (bf16[256,1024]{1,0:T(8,128)(2,1)}, bf16[256,1024]{1,0:T(8,128)(2,1)}, u32[]{:S(2)}, u32[]{:S(2)}) collective-permute-start(bf16[256,1024]{1,0:T(8,128)(2,1)} %convolution_convert_fusion.7), channel_id=1, source_target_pairs={{0,1},{1,0},{2,3},{3,2},{4,5},{5,4},{6,7},{7,6},{8,9},{9,8},{10,11... | collective-permute-start | bytes 1572872 | tf_op jit(solution)/shard_map/ppermute | solution.py:23
  168.3 4.6 %copy-start.25 = (bf16[512,1024]{1,0:T(8,128)(2,1)S(1)}, bf16[512,1024]{1,0:T(8,128)(2,1)}, u32[]{:S(2)}) copy-start(bf16[512,1024]{1,0:T(8,128)(2,1)} %copy-done.24) | copy-start | bytes 3145732
  168.3 14.2 %collective-permute-start.14 = (bf16[256,1024]{1,0:T(8,128)(2,1)}, bf16[256,1024]{1,0:T(8,128)(2,1)}, u32[]{:S(2)}, u32[]{:S(2)}) collective-permute-start(bf16[256,1024]{1,0:T(8,128)(2,1)} %fusion.9), channel_id=1, source_target_pairs={{0,4},{4,0},{1,5},{5,1},{2,6},{6,2},{3,7},{7,3},{8,12},{12,8},{9,1... | collective-permute-start | bytes 1572872 | tf_op jit(solution)/shard_map/ppermute | solution.py:23
  171.0 4.3 %collective-permute-start.15 = (bf16[256,1024]{1,0:T(8,128)(2,1)}, bf16[256,1024]{1,0:T(8,128)(2,1)}, u32[]{:S(2)}, u32[]{:S(2)}) collective-permute-start(bf16[256,1024]{1,0:T(8,128)(2,1)} %convolution_convert_fusion.5), channel_id=1, source_target_pairs={{0,1},{1,0},{2,3},{3,2},{4,5},{5,4},{6,7},{7,6},{8,9},{9,8},{10,11... | collective-permute-start | bytes 1572872 | tf_op jit(solution)/shard_map/ppermute | solution.py:23
  172.3 5.8 %collective-permute-start.16 = (bf16[256,1024]{1,0:T(8,128)(2,1)}, bf16[256,1024]{1,0:T(8,128)(2,1)}, u32[]{:S(2)}, u32[]{:S(2)}) collective-permute-start(bf16[256,1024]{1,0:T(8,128)(2,1)} %convolution_convert_fusion.4), channel_id=1, source_target_pairs={{0,1},{1,0},{2,3},{3,2},{4,5},{5,4},{6,7},{7,6},{8,9},{9,8},{10,11... | collective-permute-start | bytes 1572872 | tf_op jit(solution)/shard_map/ppermute | solution.py:23
  182.4 75.7 %reduce-scatter.7.cloned.1.call-start = ((), (), s32[]{:S(2)}) async-start(), calls=%async_computation.9 | async-start | bytes 1310720 | tf_op jit(solution)/shard_map/reduce_scatter | solution.py:97
  182.5 7.1 %copy-start.20 = (bf16[1,512,1024]{2,1,0:T(8,128)(2,1)S(1)}, bf16[1,512,1024]{2,1,0:T(8,128)(2,1)}, u32[]{:S(2)}) copy-start(bf16[1,512,1024]{2,1,0:T(8,128)(2,1)} %param.29) | copy-start | bytes 3145732
  185.5 6.0 %copy-start.27 = (bf16[512,512]{1,0:T(8,128)(2,1)S(1)}, bf16[512,512]{1,0:T(8,128)(2,1)}, u32[]{:S(2)}) copy-start(bf16[512,512]{1,0:T(8,128)(2,1)} %copy-done.26) | copy-start | bytes 1572868
  185.5 13.3 %collective-permute-start.17 = (bf16[256,1024]{1,0:T(8,128)(2,1)}, bf16[256,1024]{1,0:T(8,128)(2,1)}, u32[]{:S(2)}, u32[]{:S(2)}) collective-permute-start(bf16[256,1024]{1,0:T(8,128)(2,1)} %fusion.14), channel_id=1, source_target_pairs={{0,2},{1,3},{2,0},{3,1},{4,6},{5,7},{6,4},{7,5},{8,10},{9,11},{10,... | collective-permute-start | bytes 1572872 | tf_op jit(solution)/shard_map/ppermute | solution.py:23
  187.0 13.0 %collective-permute-start.18 = (bf16[256,1024]{1,0:T(8,128)(2,1)}, bf16[256,1024]{1,0:T(8,128)(2,1)}, u32[]{:S(2)}, u32[]{:S(2)}) collective-permute-start(bf16[256,1024]{1,0:T(8,128)(2,1)} %fusion.11), channel_id=1, source_target_pairs={{0,4},{4,0},{1,5},{5,1},{2,6},{6,2},{3,7},{7,3},{8,12},{12,8},{9,1... | collective-permute-start | bytes 1572872 | tf_op jit(solution)/shard_map/ppermute | solution.py:23
  202.2 2.3 collective-permute-start.19
  203.7 77.0 %reduce-scatter.9.cloned.1.call-start = ((), (), s32[]{:S(2)}) async-start(), calls=%async_computation.10 | async-start | bytes 983040 | tf_op jit(solution)/shard_map/reduce_scatter | solution.py:97
  219.9 5.6 %collective-permute-start.20 = (bf16[512,128]{1,0:T(8,128)(2,1)S(1)}, bf16[512,128]{1,0:T(8,128)(2,1)S(1)}, u32[]{:S(2)}, u32[]{:S(2)}) collective-permute-start(bf16[512,128]{1,0:T(8,128)(2,1)S(1)} %constant_dynamic-slice_fusion), channel_id=1, source_target_pairs={{0,4},{4,0},{1,5},{5,1},{2,6},{6,2},{3,7},{7,3},{8,12},{12,8},{9,1... | collective-permute-start | bytes 393224 | tf_op jit(solution)/shard_map/ppermute | solution.py:23
  222.0 3.6 %copy-start.6 = (bf16[1024,384]{1,0:T(8,128)(2,1)S(1)}, bf16[1024,384]{1,0:T(8,128)(2,1)}, u32[]{:S(2)}) copy-start(bf16[1024,384]{1,0:T(8,128)(2,1)} %copy-done.5) | copy-start | bytes 2359300
  224.1 25.6 %collective-permute-start.25 = (bf16[256,1024]{1,0:T(8,128)(2,1)}, bf16[256,1024]{1,0:T(8,128)(2,1)}, u32[]{:S(2)}, u32[]{:S(2)}) collective-permute-start(bf16[256,1024]{1,0:T(8,128)(2,1)} %add_convert_fusion.6), channel_id=1, source_target_pairs={{0,2},{1,3},{2,0},{3,1},{4,6},{5,7},{6,4},{7,5},{8,10},{9,11},{10,... | collective-permute-start | bytes 1572872 | tf_op jit(solution)/shard_map/ppermute | solution.py:23
  233.9 3.1 collective-permute-start.21
  233.9 9.0 %collective-permute-start.22 = (bf16[512,256]{1,0:T(8,128)(2,1)}, bf16[512,256]{1,0:T(8,128)(2,1)}, u32[]{:S(2)}, u32[]{:S(2)}) collective-permute-start(bf16[512,256]{1,0:T(8,128)(2,1)} %bitcast.37), channel_id=1, source_target_pairs={{0,4},{4,0},{1,5},{5,1},{2,6},{6,2},{3,7},{7,3},{8,12},{12,8},{9,1... | collective-permute-start | bytes 786440 | tf_op jit(solution)/shard_map/ppermute | solution.py:23
  236.6 11.6 %collective-permute-start.24 = (bf16[256,1024]{1,0:T(8,128)(2,1)}, bf16[256,1024]{1,0:T(8,128)(2,1)}, u32[]{:S(2)}, u32[]{:S(2)}) collective-permute-start(bf16[256,1024]{1,0:T(8,128)(2,1)} %convolution_convert_fusion.1), channel_id=1, source_target_pairs={{0,1},{1,0},{2,3},{3,2},{4,5},{5,4},{6,7},{7,6},{8,9},{9,8},{10,11... | collective-permute-start | bytes 1572872 | tf_op jit(solution)/shard_map/ppermute | solution.py:23
  243.0 13.9 %collective-permute-start.23 = (bf16[256,1024]{1,0:T(8,128)(2,1)}, bf16[256,1024]{1,0:T(8,128)(2,1)}, u32[]{:S(2)}, u32[]{:S(2)}) collective-permute-start(bf16[256,1024]{1,0:T(8,128)(2,1)} %add_convert_fusion.8), channel_id=1, source_target_pairs={{0,4},{4,0},{1,5},{5,1},{2,6},{6,2},{3,7},{7,3},{8,12},{12,8},{9,1... | collective-permute-start | bytes 1572872 | tf_op jit(solution)/shard_map/ppermute | solution.py:23
  258.1 7.5 %copy-start.42 = (bf16[256,512]{1,0:T(8,128)(2,1)S(1)}, bf16[256,512]{1,0:T(8,128)(2,1)}, u32[]{:S(2)}) copy-start(bf16[256,512]{1,0:T(8,128)(2,1)} %reduce-scatter.5.cloned.1.call-done) | copy-start | bytes 786436
  258.1 7.5 %copy-start.43 = (bf16[256,512]{1,0:T(8,128)(2,1)S(1)}, bf16[256,512]{1,0:T(8,128)(2,1)}, u32[]{:S(2)}) copy-start(bf16[256,512]{1,0:T(8,128)(2,1)} %reduce-scatter.7.cloned.1.call-done) | copy-start | bytes 786436
  258.1 14.6 %collective-permute-start.26 = (bf16[256,1024]{1,0:T(8,128)(2,1)S(1)}, bf16[256,1024]{1,0:T(8,128)(2,1)S(1)}, u32[]{:S(2)}, u32[]{:S(2)}) collective-permute-start(bf16[256,1024]{1,0:T(8,128)(2,1)S(1)} %add_convert_fusion.5), channel_id=1, source_target_pairs={{0,2},{1,3},{2,0},{3,1},{4,6},{5,7},{6,4},{7,5},{8,10},{9,11},{10,... | collective-permute-start | bytes 1572872 | tf_op jit(solution)/shard_map/ppermute | solution.py:23
  262.0 10.8 %all-to-all-start.1 = ((f32[8,32,128]{2,1,0:T(8,128)}), f32[8,32,128]{2,1,0:T(8,128)S(1)}, u32[]{:S(2)}, u32[]{:S(2)}) async-start(f32[8,32,128]{2,1,0:T(8,128)} %copy.96), calls=%async_computation.3 | async-start | bytes 262144 | tf_op jit(solution)/shard_map/all_to_all | solution.py:527
  265.4 35.1 %reduce-scatter.11.cloned.1.call-start = ((), (), s32[]{:S(2)}) async-start(), calls=%async_computation.11 | async-start | bytes 327680 | tf_op jit(solution)/shard_map/reduce_scatter | solution.py:97
  266.4 8.3 %collective-permute-start.30 = (bf16[2,128,512]{2,1,0:T(8,128)(2,1)}, bf16[2,128,512]{2,1,0:T(8,128)(2,1)}, u32[]{:S(2)}, u32[]{:S(2)}) collective-permute-start(bf16[2,128,512]{2,1,0:T(8,128)(2,1)} %get-tuple-element.270), channel_id=1, source_target_pairs={{0,4},{4,0},{1,5},{5,1},{2,6},{6,2},{3,7},{7,3},{8,12},{12,8},{9,1... | collective-permute-start | bytes 786440 | tf_op jit(solution)/shard_map/ppermute | solution.py:23
  273.0 15.2 %collective-permute-start.28 = (bf16[256,1024]{1,0:T(8,128)(2,1)S(1)}, bf16[256,1024]{1,0:T(8,128)(2,1)}, u32[]{:S(2)}, u32[]{:S(2)}) collective-permute-start(bf16[256,1024]{1,0:T(8,128)(2,1)S(1)} %fusion.35), channel_id=1, source_target_pairs={{0,1},{1,0},{2,3},{3,2},{4,5},{5,4},{6,7},{7,6},{8,9},{9,8},{10,11... | collective-permute-start | bytes 1572872 | tf_op jit(solution)/shard_map/ppermute | solution.py:23
  273.1 3.2 %collective-permute-start.31 = (f32[2,128]{1,0:T(2,128)S(1)}, f32[2,128]{1,0:T(2,128)S(1)}, u32[]{:S(2)}, u32[]{:S(2)}) collective-permute-start(f32[2,128]{1,0:T(2,128)S(1)} %slice.132), channel_id=1, source_target_pairs={{0,1},{1,0},{2,3},{3,2},{4,5},{5,4},{6,7},{7,6},{8,9},{9,8},{10,11... | collective-permute-start | bytes 3080 | tf_op jit(solution)/shard_map/ppermute | solution.py:23
  276.3 4.4 %collective-permute-start.32 = (f32[2,128]{1,0:T(2,128)S(1)}, f32[2,128]{1,0:T(2,128)S(1)}, u32[]{:S(2)}, u32[]{:S(2)}) collective-permute-start(f32[2,128]{1,0:T(2,128)S(1)} %slice_add_fusion), channel_id=1, source_target_pairs={{0,2},{1,3},{2,0},{3,1},{4,6},{5,7},{6,4},{7,5},{8,10},{9,11},{10,... | collective-permute-start | bytes 3080 | tf_op jit(solution)/shard_map/ppermute | solution.py:23
  279.0 23.1 %collective-permute-start.27 = (bf16[256,1024]{1,0:T(8,128)(2,1)}, bf16[256,1024]{1,0:T(8,128)(2,1)}, u32[]{:S(2)}, u32[]{:S(2)}) collective-permute-start(bf16[256,1024]{1,0:T(8,128)(2,1)} %add_convert_fusion.4), channel_id=1, source_target_pairs={{0,1},{1,0},{2,3},{3,2},{4,5},{5,4},{6,7},{7,6},{8,9},{9,8},{10,11... | collective-permute-start | bytes 1572872 | tf_op jit(solution)/shard_map/ppermute | solution.py:23
  281.7 5.3 %collective-permute-start.29 = (bf16[128,384]{1,0:T(8,128)(2,1)S(1)}, bf16[128,384]{1,0:T(8,128)(2,1)S(1)}, u32[]{:S(2)}, u32[]{:S(2)}) collective-permute-start(bf16[128,384]{1,0:T(8,128)(2,1)S(1)} %dynamic-slice_convert_fusion), channel_id=1, source_target_pairs={{0,4},{4,0},{1,5},{5,1},{2,6},{6,2},{3,7},{7,3},{8,12},{12,8},{9,1... | collective-permute-start | bytes 294920 | tf_op jit(solution)/shard_map/ppermute | solution.py:23
  289.3 14.2 %copy-start.11 = (bf16[256,1024]{1,0:T(8,128)(2,1)S(1)}, bf16[256,1024]{1,0:T(8,128)(2,1)}, u32[]{:S(2)}) copy-start(bf16[256,1024]{1,0:T(8,128)(2,1)} %copy-done.9) | copy-start | bytes 1572868
  289.3 14.2 %copy-start.14 = (bf16[256,1024]{1,0:T(8,128)(2,1)S(1)}, bf16[256,1024]{1,0:T(8,128)(2,1)}, u32[]{:S(2)}) copy-start(bf16[256,1024]{1,0:T(8,128)(2,1)} %copy-done.12) | copy-start | bytes 1572868
  (21 other events, 42.8 us)
Sparse Core Ops, SparseCore 0:
  87.8 26.1 all-gather.2
  128.6 27.8 all-gather.4
  182.6 26.6 reduce-scatter.4
  212.1 25.7 reduce-scatter.6
  248.3 22.0 reduce-scatter.8
  280.8 19.6 reduce-scatter.10

commit v2 on v0

--- a/solution.py
+++ b/solution.py
@@ -351,9 +351,9 @@
             smalls[:, 16 : 16 + up_rows, :hrow], ctx_place * (up_rows // 2), up_rows // 2, 1
         )
         up_bias = up_bias.transpose(1, 0, 2).reshape(1, -1)
-        return (vectors, up_bias), ()
-
-    attn_sum, (vectors, up_bias_part), unused = sum_tp(
+        return (vectors, up_bias, down_full), ()
+
+    attn_sum, (vectors, up_bias_part, down_full), unused = sum_tp(
         out_part, block_len, core_place, small_vectors, smalls
     )
     gain_one, shift_one, gain_two, shift_two, out_bias, down_bias = (vectors[i] for i in range(6))
@@ -368,14 +368,12 @@
         return gelu_pull(grad_activated)[0].astype(jnp.bfloat16)
 
     half_rows = lax.dynamic_slice_in_dim(normed_two, core_place * half, half, 0)
-    half_rows, late_normed, down_full = lax.optimization_barrier(
-        (half_rows, normed_two, down_full)
-    )
+    half_rows, late_normed = lax.optimization_barrier((half_rows, normed_two))
     got = swap(half_rows, "ctx")
     own_pre = hidden(late_normed)
     own_active = gelu_tanh(own_pre).astype(jnp.bfloat16)
+    other_grad = jnp.concatenate([grad_got, grad_turned])
     own_hidden = hidden_grad(own_pre, own_grad)
-    other_grad = jnp.concatenate([grad_got, grad_turned])
     got, own_hidden, own_active, other_grad = lax.optimization_barrier(
         (got, own_hidden, own_active, other_grad)
     )
@@ -440,7 +438,6 @@
     mlp_across = swap(mlp_pair, "tp", CHIP)
     kept_out, sent_out = weight_product(late_branch, attended, ctx_place)
     got_cols, kept_out, sent_out = lax.optimization_barrier((got_cols, kept_out, sent_out))
-    got_out = swap(sent_out, "ctx")
     grad_heads = jnp.concatenate(ordered(ctx_place, own_cols, got_cols))
     grad_qkv_part, bias_sums = pl.pallas_call(
         functools.partial(attend_back_kernel, rows, score_scale),
@@ -470,11 +467,10 @@
     first_sent, late_part = lax.optimization_barrier((first_sent, grad_qkv_part))
     first_got = swap(first_sent, "ctx")
     grad_qkv_weight = dot(normed_all, late_part, 0, 0).astype(jnp.bfloat16)
-    first_got, first_kept, grad_qkv_weight, kept_out, got_out, mlp_across, mlp_pair = (
-        lax.optimization_barrier(
-            (first_got, first_kept, grad_qkv_weight, kept_out, got_out, mlp_across, mlp_pair)
-        )
-    )
+    first_got, first_kept, sent_out, mlp_across, mlp_pair = lax.optimization_barrier(
+        (first_got, first_kept, sent_out, mlp_across, mlp_pair)
+    )
+    got_out = swap(sent_out, "ctx")
     grad_qkv_sum = row_major(scatter_rows(grad_qkv_weight)).astype(jnp.float32)
     own_rows = lax.dynamic_slice_in_dim(grad_qkv_sum, ctx_place * drow, drow, 0)
     sent_rows = swap(
@@ -503,7 +499,7 @@
         )
 
     def small_work(gated, chip_sum):
-        up_rows_sum, down_rows, grad_up_bias, mlp_pair, mlp_across, kept_out, got_out = gated
+        up_rows_sum, down_rows, grad_up_bias, mlp_pair, mlp_across, kept_out = gated
         ffn_rows = jnp.stack([up_rows_sum, down_rows]).reshape(2, 2, drow, part_hidden)
         ffn_kept, ffn_sent = ordered(ctx_place, ffn_rows[:, 0], ffn_rows[:, 1])
         ffn_got = swap(ffn_sent, "ctx")
@@ -538,7 +534,7 @@
     first_pair, gated = lax.optimization_barrier(
         (
             first_pair,
-            (up_rows_sum, down_rows, grad_up_bias, mlp_pair, mlp_across, kept_out, got_out),
+            (up_rows_sum, down_rows, grad_up_bias, mlp_pair, mlp_across, kept_out),
         )
     )
     first_across = swap(first_pair, "tp", CHIP)

time: 309 us -> 296 us (0.958)
  other arithmetic: 56.4 us -> 43.5 us
  starting transfers between devices: 36.9 us -> 49.2 us
  waiting for transfers between devices: 118 us -> 110 us
    ppermute x33, waiting for transfers between devices: 70.2 us -> 51.6 us  [swap(): return lax.ppermute(array, axis, [(i, i ^ mask) for i in range(devices)])]
    all_to_all x1, waiting for transfers between devices: 5.46 us -> 17.4 us  [gather_fsdp(): lax.all_to_all(jnp.broadcast_to(block[None], (devices,) + block.shape), '...]
    reduce_scatter x4, starting transfers between devices: 0.63 us -> 12.1 us  [scatter_rows(): return lax.psum_scatter(array, 'fsdp', scatter_dimension=0, tiled=True)]
    reduce_sum x1, other arithmetic: 11 us -> 2.92 us  [local(): grad_out_bias = jnp.sum(grad_branch_low.astype(jnp.float32), axis=0)]
    unnamed x97 -> x95, local copies, waits for them, and re-layouts: 10.1 us -> 9.53 us
  transfers between devices with their start and end apart: 41 -> 41, of which waited for: 21 -> 23; matrix products, arithmetic and copies ran while one was open for 33% -> 28% of each run, Pallas kernels for 5% -> 5%
where the time goes in v2:
time: 296 us; the launch traced here: 293 us
  waiting for transfers between devices  110 us (37%)
  starting transfers between devices  49.2 us (17%)
  other arithmetic  43.5 us (15%)
  matrix products  41 us (14%)
  local copies, waits for them, and re-layouts  19.7 us (7%)
  between operations  15.4 us (5%)
  Pallas kernels  14.7 us (5%)
    ppermute x33, waiting for transfers between devices, swap(): return lax.ppermute(array, axis, [(i, i ^ mask) for i in range(devices)])  51.6 us
    dot_general x25, matrix products, dot(): lax.dot_general(left, right, (((left_dim,), (right_dim,)), ((), ())), pre...  41 us
    all_gather x2, waiting for transfers between devices, gather_rows(): return lax.all_gather(block, 'fsdp', axis=0, tiled=True)  30 us
    ppermute x33, starting transfers between devices, swap(): return lax.ppermute(array, axis, [(i, i ^ mask) for i in range(devices)])  28.2 us
    all_to_all x1, waiting for transfers between devices, gather_fsdp(): lax.all_to_all(jnp.broadcast_to(block[None], (devices,) + block.shape), '...  17.4 us
    reduce_scatter x4, starting transfers between devices, scatter_rows(): return lax.psum_scatter(array, 'fsdp', scatter_dimension=0, tiled=True)  12.1 us
    reduce_scatter x4, waiting for transfers between devices, scatter_rows(): return lax.psum_scatter(array, 'fsdp', scatter_dimension=0, tiled=True)  10.3 us
    unnamed x95, local copies, waits for them, and re-layouts  9.53 us
  transfers between devices with their start and end apart: 41, of which 23 were waited for; matrix products, arithmetic and copies ran while one was open for 28% of the time, Pallas kernels for 5%

profile of v2, /device:TPU:0, one launch (start us, length us, event | category | flops | bytes accessed | tf_op | source)
XLA Modules:
  0.0 293.3 jit_solution(16772556736974698209)
XLA Ops:
  10.8 3.0 %collective-permute-start = (bf16[672,128]{1,0:T(8,128)(2,1)S(1)}, bf16[672,128]{1,0:T(8,128)(2,1)S(1)}, u32[]{:S(2)}, u32[]{:S(2)}) collective-permute-start(bf16[672,128]{1,0:T(8,128)(2,1)S(1)} %pad_maximum_fusion.14), channel_id=1, source_target_pairs={{0,4},{4,0},{1,5},{5,1},{2,6},{6,2},{3,7},{7,3},{8,12},{12,8},{9,1... | collective-permute-start | bytes 516104 | tf_op jit(solution)/shard_map/ppermute | solution.py:23
  13.8 4.4 %collective-permute-done = bf16[672,128]{1,0:T(8,128)(2,1)S(1)} collective-permute-done((bf16[672,128]{1,0:T(8,128)(2,1)S(1)}, bf16[672,128]{1,0:T(8,128)(2,1)S(1)}, u32[]{:S(2)}, u32[]{:S(2)}) %collective-permute-start) | collective-permute-done | bytes 172064 | tf_op jit(solution)/shard_map/ppermute | solution.py:23
  19.2 1.8 collective-permute-start.1
  21.2 1.3 broadcast_in_dim.14
  22.5 4.9 %all-to-all-start = ((bf16[4,2,672,128]{3,2,1,0:T(8,128)(2,1)}), bf16[4,2,672,128]{3,2,1,0:T(8,128)(2,1)}, u32[]{:S(2)}, u32[]{:S(2)}) async-start(bf16[4,2,672,128]{3,2,1,0:T(8,128)(2,1)} %broadcast_in_dim.14), calls=%async_computation | async-start | bytes 2752512 | tf_op jit(solution)/shard_map/all_to_all | solution.py:32
  27.3 5.1 %collective-permute-done.1 = bf16[256,1024]{1,0:T(8,128)(2,1)S(1)} collective-permute-done((bf16[256,1024]{1,0:T(8,128)(2,1)S(1)}, bf16[256,1024]{1,0:T(8,128)(2,1)S(1)}, u32[]{:S(2)}, u32[]{:S(2)}) %collective-permute-start.1) | collective-permute-done | bytes 524320 | tf_op jit(solution)/shard_map/ppermute | solution.py:23
  32.6 1.5 collective-permute-start.3
  34.4 1.9 broadcast_select_fusion.1
  38.4 1.4 collective-permute-start.5
  39.8 1.6 collective-permute-done.3
  41.6 17.4 %all-to-all-done = bf16[4,2,672,128]{3,2,1,0:T(8,128)(2,1)} async-done(((bf16[4,2,672,128]{3,2,1,0:T(8,128)(2,1)}), bf16[4,2,672,128]{3,2,1,0:T(8,128)(2,1)}, u32[]{:S(2)}, u32[]{:S(2)}) %all-to-all-start) | async-done | bytes 1376288 | tf_op jit(solution)/shard_map/all_to_all | solution.py:32
  61.3 7.7 %shard_map.254 = (bf16[1024,1024]{1,0:T(8,128)(2,1)S(1)}, bf16[1024,384]{1,0:T(8,128)(2,1)S(1)}, bf16[1024,128]{1,0:T(8,128)(2,1)S(1)}, bf16[1024,384]{1,0:T(8,128)(2,1)S(1)}, bf16[1024,256]{1,0:T(8,128)(2,1)S(1)}) custom-call(bf16[1024,1024]{1,0:T(8,128)(2,1)S(1)} %pad_maximum_fusion.tokens_ref, bf16[8,672,128]{2,1,0:T(8,128)(2,1)} %bitcast.19.packs_ref, ...), custom_call_target="tpu_custom_call" | custom-call | flops 805306368 | bytes 8388608 | tf_op jit(solution)/shard_map/pallas_call | solution.py:314
  69.8 1.3 copy-done.4
  73.7 5.0 %collective-permute-done.4 = bf16[512,128]{1,0:T(8,128)(2,1)S(1)} collective-permute-done((bf16[512,128]{1,0:T(8,128)(2,1)S(1)}, bf16[512,128]{1,0:T(8,128)(2,1)S(1)}, u32[]{:S(2)}, u32[]{:S(2)}) %collective-permute-start.4) | collective-permute-done | bytes 131104 | tf_op jit(solution)/shard_map/ppermute | solution.py:23
  79.7 6.4 %all-gather.3.cloned.1.call-done = bf16[1024,512]{1,0:T(8,128)(2,1)} async-done(((bf16[256,512]{1,0:T(8,128)(2,1)}), bf16[1024,512]{1,0:T(8,128)(2,1)}) %all-gather.3.cloned.1.call-update) | async-done | bytes 1048592 | tf_op jit(solution)/shard_map/all_gather | solution.py:38
  86.2 1.4 convolution_convert_fusion.8
  87.7 1.9 collective-permute-done.7
  89.9 1.5 collective-permute-start.8
  92.2 23.5 %all-gather.5.cloned.1.call-done = bf16[1024,512]{1,0:T(8,128)(2,1)} async-done(((bf16[256,512]{1,0:T(8,128)(2,1)}), bf16[1024,512]{1,0:T(8,128)(2,1)}) %all-gather.5.cloned.1.call-update) | async-done | bytes 1048592 | tf_op jit(solution)/shard_map/all_gather | solution.py:38
  116.0 1.3 pad_maximum_fusion.2
  120.5 1.5 collective-permute-start.10
  122.7 2.5 multiply_convert_fusion.1
  125.2 9.3 %collective-permute-done.10 = bf16[256,1024]{1,0:T(8,128)(2,1)S(1)} collective-permute-done((bf16[256,1024]{1,0:T(8,128)(2,1)S(1)}, bf16[256,1024]{1,0:T(8,128)(2,1)S(1)}, u32[]{:S(2)}, u32[]{:S(2)}) %collective-permute-start.10) | collective-permute-done | bytes 524320 | tf_op jit(solution)/shard_map/ppermute | solution.py:23
  136.4 2.3 multiply_convert_fusion
  140.1 1.5 dynamic-slice_reduce_fusion
  141.6 2.7 convolution_convert_fusion.7
  144.7 2.3 fusion.9
  147.0 1.5 collective-permute-start.14
  148.5 1.3 convolution_convert_fusion.5
  149.8 1.3 convolution_convert_fusion.4
  152.4 1.8 add_convert_fusion.2
  154.1 2.8 fusion.10
  157.0 2.4 fusion.11
  159.4 2.0 collective-permute-done.14
  161.4 11.6 %reduce-scatter.7.cloned.1.call-start = ((), (), s32[]{:S(2)}) async-start(), calls=%async_computation.9 | async-start | bytes 1310720 | tf_op jit(solution)/shard_map/reduce_scatter | solution.py:97
  173.0 3.0 %fusion.14 = bf16[256,1024]{1,0:T(8,128)(2,1)} fusion(bf16[1024,512]{1,0:T(8,128)(2,1)} %all-gather.3.cloned.1.call-done, bf16[256,1024]{1,0:T(8,128)(2,1)} %collective-permute-done.14, bf16[256,1024]{1,0:T(8,128)(2,1)} %collective-permute-done.11, bf16[512,512]{1,0:T(8,128)(2,1)} %get-tuple-element.133, s32[]{:T(128)S(6)} %select_n.252), kind=kOutput, calls=%fused_computation.59 | convolution fusion | flops 270270464 | bytes 2883588 | tf_op jit(solution)/shard_map/dot_general | solution.py:126
  175.9 1.5 collective-permute-start.17
  177.4 1.5 collective-permute-start.18
  180.1 1.9 fusion.77
  182.3 1.7 add_convert_fusion.1
  184.0 5.4 %collective-permute-done.17 = bf16[256,1024]{1,0:T(8,128)(2,1)} collective-permute-done((bf16[256,1024]{1,0:T(8,128)(2,1)}, bf16[256,1024]{1,0:T(8,128)(2,1)}, u32[]{:S(2)}, u32[]{:S(2)}) %collective-permute-start.17) | collective-permute-done | bytes 524320 | tf_op jit(solution)/shard_map/ppermute | solution.py:23
  190.6 2.2 add_convert_fusion.9
  192.8 1.5 multiply_reduce_fusion.3
  195.1 1.3 broadcast_select_fusion.7
  196.4 2.6 fusion.6
  199.0 2.9 convert_reduce_fusion.2
  202.4 1.5 collective-permute-start.20
  204.4 2.1 add_convert_fusion.6
  208.1 7.0 %shard_map.255 = (bf16[1024,384]{1,0:T(8,128)(2,1)S(1)}, f32[2,128]{1,0:T(2,128)S(1)}) custom-call(bf16[1024,384]{1,0:T(8,128)(2,1)S(1)} %copy-done.6, bf16[1024,128]{1,0:T(8,128)(2,1)S(1)} %pad_maximum_fusion.10.grad_ref, s32[1,1024]{1,0:T(1,128)S(1)} %copy-done.3, s32[1024,1]{1,0:T(8,128)S(1)} %copy.91.seg_col_ref), custom_call_target="tpu_custom_call" | custom-call | flops 1342177280 | bytes 2097152 | tf_op jit(solution)/shard_map/pallas_call | solution.py:442
  219.8 1.5 collective-permute-start.22
  221.2 3.8 %convolution_convert_fusion = bf16[1024,384]{1,0:T(8,128)(2,1)} fusion(bf16[1024,1024]{1,0:T(8,128)(2,1)} %copy-done.4, bf16[1024,384]{1,0:T(8,128)(2,1)S(1)} %get-tuple-element.168), kind=kOutput, calls=%fused_computation.38 | convolution fusion | flops 805699584 | bytes 3670016 | tf_op jit(solution)/shard_map/dot_general | solution.py:126
  225.0 1.5 add_convert_fusion.7
  226.6 7.5 %collective-permute-done.22 = bf16[256,1024]{1,0:T(8,128)(2,1)} collective-permute-done((bf16[256,1024]{1,0:T(8,128)(2,1)}, bf16[256,1024]{1,0:T(8,128)(2,1)}, u32[]{:S(2)}, u32[]{:S(2)}) %collective-permute-start.22) | collective-permute-done | bytes 524320 | tf_op jit(solution)/shard_map/ppermute | solution.py:23
  234.1 1.5 collective-permute-start.26
  237.4 1.5 fusion.27
  239.9 4.0 %all-to-all-start.1 = ((f32[8,32,128]{2,1,0:T(8,128)}), f32[8,32,128]{2,1,0:T(8,128)S(1)}, u32[]{:S(2)}, u32[]{:S(2)}) async-start(f32[8,32,128]{2,1,0:T(8,128)} %copy.96), calls=%async_computation.3 | async-start | bytes 262144 | tf_op jit(solution)/shard_map/all_to_all | solution.py:528
  244.1 1.8 select_bitcast_fusion
  245.9 2.0 collective-permute-start.30
  247.9 2.2 add_convert_fusion.4
  252.1 1.7 collective-permute-done.30
  262.5 3.5 %collective-permute-done.29 = bf16[128,384]{1,0:T(8,128)(2,1)S(1)} collective-permute-done((bf16[128,384]{1,0:T(8,128)(2,1)S(1)}, bf16[128,384]{1,0:T(8,128)(2,1)S(1)}, u32[]{:S(2)}, u32[]{:S(2)}) %collective-permute-start.29) | collective-permute-done | bytes 98336 | tf_op jit(solution)/shard_map/ppermute | solution.py:23
  269.2 10.2 %reduce-scatter.11.cloned.1.call-done = bf16[128,256]{1,0:T(8,128)(2,1)} async-done(((bf16[512,256]{1,0:T(8,128)(2,1)}), bf16[128,256]{1,0:T(8,128)(2,1)}) %reduce-scatter.11.cloned.1.call-update) | async-done | bytes 65552 | tf_op jit(solution)/shard_map/reduce_scatter | solution.py:97
  281.1 1.4 broadcast_select_fusion.5
  283.0 3.3 %add_bitcast_fusion = (f32[1,512,1024]{2,1,0:T(8,128)}, bf16[1,512,1024]{2,1,0:T(8,128)(2,1)}) fusion(f32[512,1024]{1,0:T(8,128)S(1)} %copy-done.24, bf16[512,1024]{1,0:T(8,128)(2,1)S(1)} %bitcast.163, f32[512]{0:T(512)S(1)} %broadcast_multiply_fusion, f32[512]{0:T(512)S(1)} %broadcast_multiply_fusion.1, f32[1024]{0:T(1024)S(1)} %bitcast.194, ...), kind=kLoop, calls=%fused_computation.13 | loop fusion | flops 13631488 | bytes 9457664 | tf_op jit(solution)/shard_map/broadcast_in_dim | solution.py:566
  (253 shorter events, 53.6 us)
Async XLA Ops:
  10.8 7.4 %collective-permute-start = (bf16[672,128]{1,0:T(8,128)(2,1)S(1)}, bf16[672,128]{1,0:T(8,128)(2,1)S(1)}, u32[]{:S(2)}, u32[]{:S(2)}) collective-permute-start(bf16[672,128]{1,0:T(8,128)(2,1)S(1)} %pad_maximum_fusion.14), channel_id=1, source_target_pairs={{0,4},{4,0},{1,5},{5,1},{2,6},{6,2},{3,7},{7,3},{8,12},{12,8},{9,1... | collective-permute-start | bytes 516104 | tf_op jit(solution)/shard_map/ppermute | solution.py:23
  19.2 13.2 %collective-permute-start.1 = (bf16[256,1024]{1,0:T(8,128)(2,1)S(1)}, bf16[256,1024]{1,0:T(8,128)(2,1)S(1)}, u32[]{:S(2)}, u32[]{:S(2)}) collective-permute-start(bf16[256,1024]{1,0:T(8,128)(2,1)S(1)} %constant_dynamic-slice_fusion.6), channel_id=1, source_target_pairs={{0,4},{4,0},{1,5},{5,1},{2,6},{6,2},{3,7},{7,3},{8,12},{12,8},{9,1... | collective-permute-start | bytes 1572872 | tf_op jit(solution)/shard_map/ppermute | solution.py:23
  21.1 11.3 %copy-start.41 = (bf16[1024,128]{1,0:T(8,128)(2,1)S(1)}, bf16[1024,128]{1,0:T(8,128)(2,1)}, u32[]{:S(2)}) copy-start(bf16[1024,128]{1,0:T(8,128)(2,1)} %param.23) | copy-start | bytes 786436
  21.2 11.4 %copy-start.39 = (bf16[128,1024]{1,0:T(8,128)(2,1)S(1)}, bf16[128,1024]{1,0:T(8,128)(2,1)}, u32[]{:S(2)}) copy-start(bf16[128,1024]{1,0:T(8,128)(2,1)} %param.21) | copy-start | bytes 786436
  22.5 36.6 %all-to-all-start = ((bf16[4,2,672,128]{3,2,1,0:T(8,128)(2,1)}), bf16[4,2,672,128]{3,2,1,0:T(8,128)(2,1)}, u32[]{:S(2)}, u32[]{:S(2)}) async-start(bf16[4,2,672,128]{3,2,1,0:T(8,128)(2,1)} %broadcast_in_dim.14), calls=%async_computation | async-start | bytes 2752512 | tf_op jit(solution)/shard_map/all_to_all | solution.py:32
  27.3 7.1 %copy-start.7 = (bf16[1,512,1024]{2,1,0:T(8,128)(2,1)S(1)}, bf16[1,512,1024]{2,1,0:T(8,128)(2,1)}, u32[]{:S(2)}) copy-start(bf16[1,512,1024]{2,1,0:T(8,128)(2,1)} %param.15) | copy-start | bytes 3145732
  27.3 58.8 %all-gather.3.cloned.1.call-start = ((), (), s32[]{:S(2)}) async-start(), calls=%async_computation.6 | async-start | bytes 1310720 | tf_op jit(solution)/shard_map/all_gather | solution.py:38
  32.4 1.9 collective-permute-start.2
  32.6 8.8 %collective-permute-start.3 = (bf16[256,512]{1,0:T(8,128)(2,1)S(1)}, bf16[256,512]{1,0:T(8,128)(2,1)S(1)}, u32[]{:S(2)}, u32[]{:S(2)}) collective-permute-start(bf16[256,512]{1,0:T(8,128)(2,1)S(1)} %fusion.34), channel_id=1, source_target_pairs={{0,4},{4,0},{1,5},{5,1},{2,6},{6,2},{3,7},{7,3},{8,12},{12,8},{9,1... | collective-permute-start | bytes 786440 | tf_op jit(solution)/shard_map/ppermute | solution.py:23
  36.3 5.1 %copy-start.40 = (bf16[128,1024]{1,0:T(8,128)(2,1)S(1)}, bf16[128,1024]{1,0:T(8,128)(2,1)}, u32[]{:S(2)}) copy-start(bf16[128,1024]{1,0:T(8,128)(2,1)} %param.21) | copy-start | bytes 786436
  38.4 21.6 %copy-start.3 = (s32[1,1024]{1,0:T(1,128)S(1)}, s32[1,1024]{1,0:T(1,128)}, u32[]{:S(2)}) copy-start(s32[1,1024]{1,0:T(1,128)} %seg_row_ref.3) | copy-start | bytes 12292
  38.4 21.8 %collective-permute-start.5 = (bf16[256,1024]{1,0:T(8,128)(2,1)}, bf16[256,1024]{1,0:T(8,128)(2,1)}, u32[]{:S(2)}, u32[]{:S(2)}) collective-permute-start(bf16[256,1024]{1,0:T(8,128)(2,1)} %constant_dynamic-slice_fusion.2), channel_id=1, source_target_pairs={{0,4},{4,0},{1,5},{5,1},{2,6},{6,2},{3,7},{7,3},{8,12},{12,8},{9,1... | collective-permute-start | bytes 1572872 | tf_op jit(solution)/shard_map/ppermute | solution.py:23
  59.9 55.9 %all-gather.5.cloned.1.call-start = ((), (), s32[]{:S(2)}) async-start(), calls=%async_computation.7 | async-start | bytes 1310720 | tf_op jit(solution)/shard_map/all_gather | solution.py:38
  60.2 19.5 %collective-permute-start.6 = (bf16[256,1024]{1,0:T(8,128)(2,1)}, bf16[256,1024]{1,0:T(8,128)(2,1)}, u32[]{:S(2)}, u32[]{:S(2)}) collective-permute-start(bf16[256,1024]{1,0:T(8,128)(2,1)} %collective-permute-done.5), channel_id=1, source_target_pairs={{0,1},{1,0},{2,3},{3,2},{4,5},{5,4},{6,7},{7,6},{8,9},{9,8},{10,11... | collective-permute-start | bytes 1572872 | tf_op jit(solution)/shard_map/ppermute | solution.py:23
  72.7 16.8 %copy-start.1 = (bf16[1024,256]{1,0:T(8,128)(2,1)S(1)}, bf16[1024,256]{1,0:T(8,128)(2,1)}, u32[]{:S(2)}) copy-start(bf16[1024,256]{1,0:T(8,128)(2,1)} %copy-done) | copy-start | bytes 1572868
  72.8 6.0 %collective-permute-start.4 = (bf16[512,128]{1,0:T(8,128)(2,1)S(1)}, bf16[512,128]{1,0:T(8,128)(2,1)S(1)}, u32[]{:S(2)}, u32[]{:S(2)}) collective-permute-start(bf16[512,128]{1,0:T(8,128)(2,1)S(1)} %constant_dynamic-slice_fusion.3), channel_id=1, source_target_pairs={{0,4},{4,0},{1,5},{5,1},{2,6},{6,2},{3,7},{7,3},{8,12},{12,8},{9,1... | collective-permute-start | bytes 393224 | tf_op jit(solution)/shard_map/ppermute | solution.py:23
  73.4 163.4 %reduce-scatter.5.cloned.1.call-start = ((), (), s32[]{:S(2)}) async-start(), calls=%async_computation.8 | async-start | bytes 1310720 | tf_op jit(solution)/shard_map/reduce_scatter | solution.py:97
  87.6 2.0 collective-permute-start.7
  89.9 25.8 %collective-permute-start.8 = (bf16[256,1024]{1,0:T(8,128)(2,1)S(1)}, bf16[256,1024]{1,0:T(8,128)(2,1)S(1)}, u32[]{:S(2)}, u32[]{:S(2)}) collective-permute-start(bf16[256,1024]{1,0:T(8,128)(2,1)S(1)} %add_convert_fusion.11), channel_id=1, source_target_pairs={{0,2},{1,3},{2,0},{3,1},{4,6},{5,7},{6,4},{7,5},{8,10},{9,11},{10,... | collective-permute-start | bytes 1572872 | tf_op jit(solution)/shard_map/ppermute | solution.py:23
  92.2 25.2 %copy-start.43 = (f32[8,1024]{1,0:T(8,128)S(1)}, f32[8,1024]{1,0:T(8,128)}, u32[]{:S(2)}) copy-start(f32[8,1024]{1,0:T(8,128)} %slice_bitcast_fusion.4) | copy-start | bytes 98308
  116.0 2.0 collective-permute-start.9
  117.4 17.1 %copy-start.31 = (bf16[512,1024]{1,0:T(8,128)(2,1)}, bf16[512,1024]{1,0:T(8,128)(2,1)S(1)}, u32[]{:S(2)}) copy-start(bf16[512,1024]{1,0:T(8,128)(2,1)S(1)} %pad_maximum_fusion.2) | copy-start | bytes 3145732
  118.0 7.2 %copy-start.9 = (bf16[256,1024]{1,0:T(8,128)(2,1)}, bf16[256,1024]{1,0:T(8,128)(2,1)S(1)}, u32[]{:S(2)}) copy-start(bf16[256,1024]{1,0:T(8,128)(2,1)S(1)} %get-tuple-element.258) | copy-start | bytes 1572868
  118.0 7.2 %copy-start.12 = (bf16[256,1024]{1,0:T(8,128)(2,1)}, bf16[256,1024]{1,0:T(8,128)(2,1)S(1)}, u32[]{:S(2)}) copy-start(bf16[256,1024]{1,0:T(8,128)(2,1)S(1)} %get-tuple-element.259) | copy-start | bytes 1572868
  120.5 14.0 %collective-permute-start.10 = (bf16[256,1024]{1,0:T(8,128)(2,1)S(1)}, bf16[256,1024]{1,0:T(8,128)(2,1)S(1)}, u32[]{:S(2)}, u32[]{:S(2)}) collective-permute-start(bf16[256,1024]{1,0:T(8,128)(2,1)S(1)} %constant_dynamic-slice_fusion.1), channel_id=1, source_target_pairs={{0,4},{4,0},{1,5},{5,1},{2,6},{6,2},{3,7},{7,3},{8,12},{12,8},{9,1... | collective-permute-start | bytes 1572872 | tf_op jit(solution)/shard_map/ppermute | solution.py:23
  134.5 1.9 collective-permute-start.12
  140.0 4.7 %collective-permute-start.13 = (bf16[256,1024]{1,0:T(8,128)(2,1)}, bf16[256,1024]{1,0:T(8,128)(2,1)}, u32[]{:S(2)}, u32[]{:S(2)}) collective-permute-start(bf16[256,1024]{1,0:T(8,128)(2,1)} %convolution_convert_fusion.6), channel_id=1, source_target_pairs={{0,1},{1,0},{2,3},{3,2},{4,5},{5,4},{6,7},{7,6},{8,9},{9,8},{10,11... | collective-permute-start | bytes 1572872 | tf_op jit(solution)/shard_map/ppermute | solution.py:23
  140.1 4.6 %copy-start.16 = (bf16[1024,512]{1,0:T(8,128)(2,1)S(1)}, bf16[1024,512]{1,0:T(8,128)(2,1)}, u32[]{:S(2)}) copy-start(bf16[1024,512]{1,0:T(8,128)(2,1)} %all-gather.3.cloned.1.call-done) | copy-start | bytes 3145732
  140.1 4.6 %copy-start.28 = (bf16[512,512]{1,0:T(8,128)(2,1)S(1)}, bf16[512,512]{1,0:T(8,128)(2,1)}, u32[]{:S(2)}) copy-start(bf16[512,512]{1,0:T(8,128)(2,1)} %copy-done.27) | copy-start | bytes 1572868
  141.6 6.9 %copy-start.18 = (bf16[1024,512]{1,0:T(8,128)(2,1)S(1)}, bf16[1024,512]{1,0:T(8,128)(2,1)}, u32[]{:S(2)}) copy-start(bf16[1024,512]{1,0:T(8,128)(2,1)} %all-gather.5.cloned.1.call-done) | copy-start | bytes 3145732
  141.6 6.9 %copy-start.38 = (bf16[512,512]{1,0:T(8,128)(2,1)S(1)}, bf16[512,512]{1,0:T(8,128)(2,1)}, u32[]{:S(2)}) copy-start(bf16[512,512]{1,0:T(8,128)(2,1)} %get-tuple-element.131) | copy-start | bytes 1572868
  144.3 5.5 %copy-start.35 = (bf16[512,512]{1,0:T(8,128)(2,1)S(1)}, bf16[512,512]{1,0:T(8,128)(2,1)}, u32[]{:S(2)}) copy-start(bf16[512,512]{1,0:T(8,128)(2,1)} %get-tuple-element.132) | copy-start | bytes 1572868
  144.3 28.6 %collective-permute-start.11 = (bf16[256,1024]{1,0:T(8,128)(2,1)}, bf16[256,1024]{1,0:T(8,128)(2,1)}, u32[]{:S(2)}, u32[]{:S(2)}) collective-permute-start(bf16[256,1024]{1,0:T(8,128)(2,1)} %convolution_convert_fusion.7), channel_id=1, source_target_pairs={{0,1},{1,0},{2,3},{3,2},{4,5},{5,4},{6,7},{7,6},{8,9},{9,8},{10,11... | collective-permute-start | bytes 1572872 | tf_op jit(solution)/shard_map/ppermute | solution.py:23
  147.0 4.6 %copy-start.26 = (bf16[512,1024]{1,0:T(8,128)(2,1)S(1)}, bf16[512,1024]{1,0:T(8,128)(2,1)}, u32[]{:S(2)}) copy-start(bf16[512,1024]{1,0:T(8,128)(2,1)} %copy-done.25) | copy-start | bytes 3145732
  147.0 4.6 %copy-start.30 = (bf16[512,512]{1,0:T(8,128)(2,1)S(1)}, bf16[512,512]{1,0:T(8,128)(2,1)}, u32[]{:S(2)}) copy-start(bf16[512,512]{1,0:T(8,128)(2,1)} %get-tuple-element.133) | copy-start | bytes 1572868
  147.0 14.3 %collective-permute-start.14 = (bf16[256,1024]{1,0:T(8,128)(2,1)}, bf16[256,1024]{1,0:T(8,128)(2,1)}, u32[]{:S(2)}, u32[]{:S(2)}) collective-permute-start(bf16[256,1024]{1,0:T(8,128)(2,1)} %fusion.9), channel_id=1, source_target_pairs={{0,4},{4,0},{1,5},{5,1},{2,6},{6,2},{3,7},{7,3},{8,12},{12,8},{9,1... | collective-permute-start | bytes 1572872 | tf_op jit(solution)/shard_map/ppermute | solution.py:23
  149.8 4.3 %collective-permute-start.15 = (bf16[256,1024]{1,0:T(8,128)(2,1)}, bf16[256,1024]{1,0:T(8,128)(2,1)}, u32[]{:S(2)}, u32[]{:S(2)}) collective-permute-start(bf16[256,1024]{1,0:T(8,128)(2,1)} %convolution_convert_fusion.5), channel_id=1, source_target_pairs={{0,1},{1,0},{2,3},{3,2},{4,5},{5,4},{6,7},{7,6},{8,9},{9,8},{10,11... | collective-permute-start | bytes 1572872 | tf_op jit(solution)/shard_map/ppermute | solution.py:23
  151.1 5.8 %collective-permute-start.16 = (bf16[256,1024]{1,0:T(8,128)(2,1)}, bf16[256,1024]{1,0:T(8,128)(2,1)}, u32[]{:S(2)}, u32[]{:S(2)}) collective-permute-start(bf16[256,1024]{1,0:T(8,128)(2,1)} %convolution_convert_fusion.4), channel_id=1, source_target_pairs={{0,1},{1,0},{2,3},{3,2},{4,5},{5,4},{6,7},{7,6},{8,9},{9,8},{10,11... | collective-permute-start | bytes 1572872 | tf_op jit(solution)/shard_map/ppermute | solution.py:23
  161.4 75.4 %reduce-scatter.7.cloned.1.call-start = ((), (), s32[]{:S(2)}) async-start(), calls=%async_computation.9 | async-start | bytes 1310720 | tf_op jit(solution)/shard_map/reduce_scatter | solution.py:97
  172.9 7.1 %copy-start.22 = (bf16[1,512,1024]{2,1,0:T(8,128)(2,1)S(1)}, bf16[1,512,1024]{2,1,0:T(8,128)(2,1)}, u32[]{:S(2)}) copy-start(bf16[1,512,1024]{2,1,0:T(8,128)(2,1)} %param.29) | copy-start | bytes 3145732
  175.9 6.0 %copy-start.29 = (bf16[512,512]{1,0:T(8,128)(2,1)S(1)}, bf16[512,512]{1,0:T(8,128)(2,1)}, u32[]{:S(2)}) copy-start(bf16[512,512]{1,0:T(8,128)(2,1)} %copy-done.27) | copy-start | bytes 1572868
  175.9 13.5 %collective-permute-start.17 = (bf16[256,1024]{1,0:T(8,128)(2,1)}, bf16[256,1024]{1,0:T(8,128)(2,1)}, u32[]{:S(2)}, u32[]{:S(2)}) collective-permute-start(bf16[256,1024]{1,0:T(8,128)(2,1)} %fusion.14), channel_id=1, source_target_pairs={{0,2},{1,3},{2,0},{3,1},{4,6},{5,7},{6,4},{7,5},{8,10},{9,11},{10,... | collective-permute-start | bytes 1572872 | tf_op jit(solution)/shard_map/ppermute | solution.py:23
  177.4 13.2 %collective-permute-start.18 = (bf16[256,1024]{1,0:T(8,128)(2,1)}, bf16[256,1024]{1,0:T(8,128)(2,1)}, u32[]{:S(2)}, u32[]{:S(2)}) collective-permute-start(bf16[256,1024]{1,0:T(8,128)(2,1)} %fusion.11), channel_id=1, source_target_pairs={{0,4},{4,0},{1,5},{5,1},{2,6},{6,2},{3,7},{7,3},{8,12},{12,8},{9,1... | collective-permute-start | bytes 1572872 | tf_op jit(solution)/shard_map/ppermute | solution.py:23
  192.8 2.3 collective-permute-start.19
  194.3 65.4 %reduce-scatter.9.cloned.1.call-start = ((), (), s32[]{:S(2)}) async-start(), calls=%async_computation.10 | async-start | bytes 983040 | tf_op jit(solution)/shard_map/reduce_scatter | solution.py:97
  202.4 5.6 %collective-permute-start.20 = (bf16[512,128]{1,0:T(8,128)(2,1)S(1)}, bf16[512,128]{1,0:T(8,128)(2,1)S(1)}, u32[]{:S(2)}, u32[]{:S(2)}) collective-permute-start(bf16[512,128]{1,0:T(8,128)(2,1)S(1)} %constant_dynamic-slice_fusion), channel_id=1, source_target_pairs={{0,4},{4,0},{1,5},{5,1},{2,6},{6,2},{3,7},{7,3},{8,12},{12,8},{9,1... | collective-permute-start | bytes 393224 | tf_op jit(solution)/shard_map/ppermute | solution.py:23
  204.4 3.7 %copy-start.6 = (bf16[1024,384]{1,0:T(8,128)(2,1)S(1)}, bf16[1024,384]{1,0:T(8,128)(2,1)}, u32[]{:S(2)}) copy-start(bf16[1024,384]{1,0:T(8,128)(2,1)} %copy-done.5) | copy-start | bytes 2359300
  206.5 20.0 %collective-permute-start.24 = (bf16[256,1024]{1,0:T(8,128)(2,1)}, bf16[256,1024]{1,0:T(8,128)(2,1)}, u32[]{:S(2)}, u32[]{:S(2)}) collective-permute-start(bf16[256,1024]{1,0:T(8,128)(2,1)} %add_convert_fusion.6), channel_id=1, source_target_pairs={{0,2},{1,3},{2,0},{3,1},{4,6},{5,7},{6,4},{7,5},{8,10},{9,11},{10,... | collective-permute-start | bytes 1572872 | tf_op jit(solution)/shard_map/ppermute | solution.py:23
  216.4 2.1 collective-permute-start.21
  217.6 7.4 %collective-permute-start.23 = (bf16[256,1024]{1,0:T(8,128)(2,1)}, bf16[256,1024]{1,0:T(8,128)(2,1)}, u32[]{:S(2)}, u32[]{:S(2)}) collective-permute-start(bf16[256,1024]{1,0:T(8,128)(2,1)} %convolution_convert_fusion.1), channel_id=1, source_target_pairs={{0,1},{1,0},{2,3},{3,2},{4,5},{5,4},{6,7},{7,6},{8,9},{9,8},{10,11... | collective-permute-start | bytes 1572872 | tf_op jit(solution)/shard_map/ppermute | solution.py:23
  219.8 14.3 %collective-permute-start.22 = (bf16[256,1024]{1,0:T(8,128)(2,1)}, bf16[256,1024]{1,0:T(8,128)(2,1)}, u32[]{:S(2)}, u32[]{:S(2)}) collective-permute-start(bf16[256,1024]{1,0:T(8,128)(2,1)} %add_convert_fusion.8), channel_id=1, source_target_pairs={{0,4},{4,0},{1,5},{5,1},{2,6},{6,2},{3,7},{7,3},{8,12},{12,8},{9,1... | collective-permute-start | bytes 1572872 | tf_op jit(solution)/shard_map/ppermute | solution.py:23
  234.1 16.0 %collective-permute-start.26 = (bf16[512,256]{1,0:T(8,128)(2,1)}, bf16[512,256]{1,0:T(8,128)(2,1)S(1)}, u32[]{:S(2)}, u32[]{:S(2)}) collective-permute-start(bf16[512,256]{1,0:T(8,128)(2,1)} %bitcast.181), channel_id=1, source_target_pairs={{0,4},{4,0},{1,5},{5,1},{2,6},{6,2},{3,7},{7,3},{8,12},{12,8},{9,1... | collective-permute-start | bytes 786440 | tf_op jit(solution)/shard_map/ppermute | solution.py:23
  236.8 7.3 %copy-start.42 = (bf16[256,512]{1,0:T(8,128)(2,1)S(1)}, bf16[256,512]{1,0:T(8,128)(2,1)}, u32[]{:S(2)}) copy-start(bf16[256,512]{1,0:T(8,128)(2,1)} %reduce-scatter.5.cloned.1.call-done) | copy-start | bytes 786436
  236.8 14.5 %collective-permute-start.25 = (bf16[256,1024]{1,0:T(8,128)(2,1)S(1)}, bf16[256,1024]{1,0:T(8,128)(2,1)S(1)}, u32[]{:S(2)}, u32[]{:S(2)}) collective-permute-start(bf16[256,1024]{1,0:T(8,128)(2,1)S(1)} %add_convert_fusion.5), channel_id=1, source_target_pairs={{0,2},{1,3},{2,0},{3,1},{4,6},{5,7},{6,4},{7,5},{8,10},{9,11},{10,... | collective-permute-start | bytes 1572872 | tf_op jit(solution)/shard_map/ppermute | solution.py:23
  239.9 11.4 %all-to-all-start.1 = ((f32[8,32,128]{2,1,0:T(8,128)}), f32[8,32,128]{2,1,0:T(8,128)S(1)}, u32[]{:S(2)}, u32[]{:S(2)}) async-start(f32[8,32,128]{2,1,0:T(8,128)} %copy.96), calls=%async_computation.3 | async-start | bytes 262144 | tf_op jit(solution)/shard_map/all_to_all | solution.py:528
  243.8 35.6 %reduce-scatter.11.cloned.1.call-start = ((), (), s32[]{:S(2)}) async-start(), calls=%async_computation.11 | async-start | bytes 327680 | tf_op jit(solution)/shard_map/reduce_scatter | solution.py:97
  245.9 7.9 %collective-permute-start.30 = (bf16[2,128,512]{2,1,0:T(8,128)(2,1)}, bf16[2,128,512]{2,1,0:T(8,128)(2,1)}, u32[]{:S(2)}, u32[]{:S(2)}) collective-permute-start(bf16[2,128,512]{2,1,0:T(8,128)(2,1)} %get-tuple-element.268), channel_id=1, source_target_pairs={{0,4},{4,0},{1,5},{5,1},{2,6},{6,2},{3,7},{7,3},{8,12},{12,8},{9,1... | collective-permute-start | bytes 786440 | tf_op jit(solution)/shard_map/ppermute | solution.py:23
  251.5 15.8 %collective-permute-start.28 = (bf16[256,1024]{1,0:T(8,128)(2,1)S(1)}, bf16[256,1024]{1,0:T(8,128)(2,1)}, u32[]{:S(2)}, u32[]{:S(2)}) collective-permute-start(bf16[256,1024]{1,0:T(8,128)(2,1)S(1)} %fusion.28), channel_id=1, source_target_pairs={{0,1},{1,0},{2,3},{3,2},{4,5},{5,4},{6,7},{7,6},{8,9},{9,8},{10,11... | collective-permute-start | bytes 1572872 | tf_op jit(solution)/shard_map/ppermute | solution.py:23
  251.6 3.7 %collective-permute-start.31 = (f32[2,128]{1,0:T(2,128)S(1)}, f32[2,128]{1,0:T(2,128)S(1)}, u32[]{:S(2)}, u32[]{:S(2)}) collective-permute-start(f32[2,128]{1,0:T(2,128)S(1)} %slice.132), channel_id=1, source_target_pairs={{0,1},{1,0},{2,3},{3,2},{4,5},{5,4},{6,7},{7,6},{8,9},{9,8},{10,11... | collective-permute-start | bytes 3080 | tf_op jit(solution)/shard_map/ppermute | solution.py:23
  255.3 4.4 %collective-permute-start.32 = (f32[2,128]{1,0:T(2,128)S(1)}, f32[2,128]{1,0:T(2,128)S(1)}, u32[]{:S(2)}, u32[]{:S(2)}) collective-permute-start(f32[2,128]{1,0:T(2,128)S(1)} %slice_add_fusion), channel_id=1, source_target_pairs={{0,2},{1,3},{2,0},{3,1},{4,6},{5,7},{6,4},{7,5},{8,10},{9,11},{10,... | collective-permute-start | bytes 3080 | tf_op jit(solution)/shard_map/ppermute | solution.py:23
  258.0 23.0 %collective-permute-start.27 = (bf16[256,1024]{1,0:T(8,128)(2,1)}, bf16[256,1024]{1,0:T(8,128)(2,1)}, u32[]{:S(2)}, u32[]{:S(2)}) collective-permute-start(bf16[256,1024]{1,0:T(8,128)(2,1)} %add_convert_fusion.4), channel_id=1, source_target_pairs={{0,1},{1,0},{2,3},{3,2},{4,5},{5,4},{6,7},{7,6},{8,9},{9,8},{10,11... | collective-permute-start | bytes 1572872 | tf_op jit(solution)/shard_map/ppermute | solution.py:23
  260.8 5.3 %collective-permute-start.29 = (bf16[128,384]{1,0:T(8,128)(2,1)S(1)}, bf16[128,384]{1,0:T(8,128)(2,1)S(1)}, u32[]{:S(2)}, u32[]{:S(2)}) collective-permute-start(bf16[128,384]{1,0:T(8,128)(2,1)S(1)} %dynamic-slice_convert_fusion), channel_id=1, source_target_pairs={{0,4},{4,0},{1,5},{5,1},{2,6},{6,2},{3,7},{7,3},{8,12},{12,8},{9,1... | collective-permute-start | bytes 294920 | tf_op jit(solution)/shard_map/ppermute | solution.py:23
  268.4 14.1 %copy-start.11 = (bf16[256,1024]{1,0:T(8,128)(2,1)S(1)}, bf16[256,1024]{1,0:T(8,128)(2,1)}, u32[]{:S(2)}) copy-start(bf16[256,1024]{1,0:T(8,128)(2,1)} %copy-done.9) | copy-start | bytes 1572868
  268.4 14.1 %copy-start.14 = (bf16[256,1024]{1,0:T(8,128)(2,1)S(1)}, bf16[256,1024]{1,0:T(8,128)(2,1)}, u32[]{:S(2)}) copy-start(bf16[256,1024]{1,0:T(8,128)(2,1)} %copy-done.12) | copy-start | bytes 1572868
  (21 other events, 40.6 us)
Sparse Core Ops, SparseCore 0:
  60.0 26.1 all-gather.2
  88.3 27.4 all-gather.4
  161.5 26.6 reduce-scatter.4
  194.4 25.8 reduce-scatter.6
  225.1 21.7 reduce-scatter.8
  259.8 19.5 reduce-scatter.10
